TPU v7x, 128 devices: a whole 4x4x4 slice. The times are simulated.
128 devices in a mesh: section: 4 (over x_hi, core), expert: 32 (over z, y, x_lo).
Axes of the slice: x: 4 (x_hi: 2, x_lo: 2; x = x_hi * 2 + x_lo), y: 4, z: 4, core: 2. Of those that a mesh axis runs over, the one named last changes fastest.
Arguments:
- layer_inputs: bfloat16 [4, 8, 512, 2048], P('section', None, 'expert'), may hold values from -6 to 6
- top_grad: bfloat16 [8, 512, 2048], P('section', 'expert'), may hold values from -6 to 6
- expert_ids: int32 [4, 8, 512, 8], P('section', None, 'expert'), may hold values from 0 to 31, all different within a row; in each aligned block of 16 rows (0 to 15, 16 to 31, ..., all dimensions but the last counted through in order) at most 5 rows name the same one
- router: bfloat16 [4, 2048, 32], P('section'), may hold values from -0.125 to 0.125
- norm_gain: bfloat16 [4, 2048], P('section'), may hold values from 0.099609375 to 1.8984375
- w_gate: bfloat16 [4, 32, 2048, 1024], P('section', 'expert'), may hold values from -0.125 to 0.125
- w_up: bfloat16 [4, 32, 2048, 1024], P('section', 'expert'), may hold values from -0.125 to 0.125
- w_down: bfloat16 [4, 32, 1024, 2048], P('section', 'expert'), may hold values from -0.1875 to 0.1875
Outputs:
- input_grads: bfloat16 [4, 8, 512, 2048], P('section', None, 'expert')
Inputs may be any that keep to these rules, and one draw needn't show every extreme that they name: `expert_ids`: each token names 8 different experts. Among the 16 tokens of one device in one micro-batch of one layer, no expert is named by more than 5 of them, and in some of these blocks one expert is named by exactly 5.
All inputs are finite; a program needn't handle non-finite values.
Results may differ from a plain program's by a relative error of at most 0.015.
Values may be sent and summed in bfloat16 or wider, within the bound.
A program may use at most 128 MiB of HBM per device.

v0:
```python
import jax
import jax.numpy as jnp
from jax import lax
from jax.sharding import PartitionSpec as P


def shifted(shard, axis, by):
    devices = lax.axis_size(axis)
    pairs = [(i, i + by) for i in range(devices) if 0 <= i + by < devices]
    return lax.ppermute(shard, axis, pairs)


def prepare(x_rows, gain):
    x_float = x_rows.astype(jnp.float32)
    inverse = lax.rsqrt(jnp.mean(x_float * x_float, axis=-1, keepdims=True) + 1e-05)
    normed = (x_float * inverse * gain).astype(jnp.bfloat16)
    return (x_float, inverse, normed)


def expert_rows(normed_rows, grad_rows, gate_w, up_w, down_w):
    gate = jnp.dot(normed_rows, gate_w, preferred_element_type=jnp.float32)
    up_rows = jnp.dot(normed_rows, up_w, preferred_element_type=jnp.float32)
    squash = jax.nn.sigmoid(gate)
    active = gate * squash
    hidden = (active * up_rows).astype(jnp.bfloat16)
    output = jnp.dot(hidden, down_w, preferred_element_type=jnp.float32)
    dprob = jnp.sum(output * grad_rows.astype(jnp.float32), axis=-1)
    dhidden = lax.dot_general(
        grad_rows, down_w, (((1,), (1,)), ((), ())), preferred_element_type=jnp.float32
    )
    dgate = (dhidden * up_rows * squash * (1.0 + gate * (1.0 - squash))).astype(jnp.bfloat16)
    dup = (dhidden * active).astype(jnp.bfloat16)
    returned = lax.dot_general(
        dgate, gate_w, (((1,), (1,)), ((), ())), preferred_element_type=jnp.float32
    )
    returned = returned + lax.dot_general(
        dup, up_w, (((1,), (1,)), ((), ())), preferred_element_type=jnp.float32
    )
    return (returned.astype(jnp.bfloat16), dprob)


def finish(x_float, inverse, normed, gain, router_layer, ids, grad_in, pair_back, pair_prob):
    logits = jnp.dot(normed, router_layer, preferred_element_type=jnp.float32)
    raised = jnp.exp(logits)
    probs = raised / jnp.sum(raised, axis=-1, keepdims=True)
    choose = (ids[..., None] == jnp.arange(router_layer.shape[1], dtype=jnp.int32)).astype(
        jnp.float32
    )
    picked = jnp.sum(probs[..., None, :] * choose, axis=-1)
    dfull = jnp.sum(pair_prob[..., None] * choose, axis=-2)
    dlogit = probs * (dfull - jnp.sum(probs * dfull, axis=-1, keepdims=True))
    router_term = jnp.dot(
        dlogit, router_layer.astype(jnp.float32).T, precision=lax.Precision.HIGHEST
    )
    dnormed = jnp.sum(picked[..., None] * pair_back, axis=-2) + router_term
    scaled = gain * dnormed
    inner = jnp.mean(x_float * scaled, axis=-1, keepdims=True)
    result = (
        grad_in.astype(jnp.float32)
        + inverse * scaled
        - x_float * inverse * inverse * inverse * inner
    )
    return result.astype(jnp.bfloat16)


def selection(ids, experts, capacity):
    pair_ids = ids.reshape(-1)
    onehot = (pair_ids[:, None] == jnp.arange(experts, dtype=jnp.int32)[None, :]).astype(jnp.int32)
    ranks = jnp.sum(onehot * (jnp.cumsum(onehot, axis=0) - 1), axis=1)
    target = pair_ids * capacity + ranks
    return (target[:, None] == jnp.arange(experts * capacity, dtype=jnp.int32)[None, :]).astype(
        jnp.bfloat16
    )


def pack_rows(select, rows, per_token):
    repeated = jnp.repeat(rows, per_token, axis=0)
    packed = lax.dot_general(
        select, repeated, (((0,), (0,)), ((), ())), preferred_element_type=jnp.float32
    )
    return packed.astype(jnp.bfloat16)


def pick_micro(values, index):
    return lax.dynamic_index_in_dim(values, index, 0, False)


def shards(layer_inputs, top_grad, expert_ids, router, norm_gain, w_gate, w_up, w_down):
    segments = lax.axis_size("section")
    experts = lax.axis_size("expert")
    segment_index = lax.axis_index("section")
    micro = layer_inputs.shape[1]
    tok_rows = layer_inputs.shape[2]
    width = layer_inputs.shape[3]
    per_token = expert_ids.shape[3]
    capacity = min(tok_rows, per_token * tok_rows // experts + max(1, tok_rows // 16))
    slots = experts * capacity
    gain = norm_gain[0].astype(jnp.float32)
    router_layer = router[0]
    gate_layer = w_gate[0, 0]
    up_layer = w_up[0, 0]
    down_layer = w_down[0, 0]
    ids_layer = expert_ids[0]
    x_layer = layer_inputs[0]
    top_full = lax.all_gather(top_grad, "section", axis=0, tiled=True)

    def advance(step, carry):
        previous, collected = carry
        arrived = shifted(previous, "section", -1)
        position = step - (segments - 1 - segment_index)
        working = jnp.logical_and(position >= 0, position < micro)
        chosen = jnp.clip(position, 0, micro - 1)
        grad_in = jnp.where(segment_index == segments - 1, pick_micro(top_full, chosen), arrived)
        ids_now = pick_micro(ids_layer, chosen)
        select = selection(ids_now, experts, capacity)
        x_float, inverse, normed = prepare(pick_micro(x_layer, chosen), gain)
        sent_normed = pack_rows(select, normed, per_token).reshape(experts, capacity, width)
        sent_grad = pack_rows(select, grad_in, per_token).reshape(experts, capacity, width)
        got_normed, got_grad = (
            lax.all_to_all(sent_normed, "expert", split_axis=0, concat_axis=0, tiled=True),
            lax.all_to_all(sent_grad, "expert", split_axis=0, concat_axis=0, tiled=True),
        )
        rows_normed = got_normed.reshape(slots, width)
        rows_grad = got_grad.reshape(slots, width)

        def run_expert(operands):
            return expert_rows(operands[0], operands[1], gate_layer, up_layer, down_layer)

        def skip_expert(operands):
            return (jnp.zeros((slots, width), jnp.bfloat16), jnp.zeros((slots,), jnp.float32))

        returned, dprob = lax.cond(working, run_expert, skip_expert, (rows_normed, rows_grad))
        back_home, prob_home = (
            lax.all_to_all(
                returned.reshape(experts, capacity, width),
                "expert",
                split_axis=0,
                concat_axis=0,
                tiled=True,
            ),
            lax.all_to_all(
                dprob.reshape(experts, capacity).astype(jnp.bfloat16),
                "expert",
                split_axis=0,
                concat_axis=0,
                tiled=True,
            ).astype(jnp.float32),
        )
        pair_back = lax.dot_general(
            select,
            back_home.reshape(slots, width),
            (((1,), (0,)), ((), ())),
            preferred_element_type=jnp.float32,
        )
        pair_back = pair_back.reshape(tok_rows, per_token, width)
        pair_prob = jnp.dot(
            select.astype(jnp.float32), prob_home.reshape(slots), precision=lax.Precision.HIGHEST
        )
        pair_prob = pair_prob.reshape(tok_rows, per_token)
        result = finish(
            x_float, inverse, normed, gain, router_layer, ids_now, grad_in, pair_back, pair_prob
        )
        retained = pick_micro(collected, chosen)
        collected = lax.dynamic_update_index_in_dim(
            collected, jnp.where(working, result, retained), chosen, 0
        )
        return (result, collected)

    start = (
        jnp.zeros((tok_rows, width), jnp.bfloat16),
        jnp.zeros((micro, tok_rows, width), jnp.bfloat16),
    )
    final_grad, collected = lax.fori_loop(0, micro + segments - 1, advance, start)
    return collected.reshape(1, micro, tok_rows, width)


def solution(mesh):
    placed = (
        P("section", None, "expert", None),
        P("section", "expert", None),
        P("section", None, "expert", None),
        P("section", None, None),
        P("section", None),
        P("section", "expert", None, None),
        P("section", "expert", None, None),
        P("section", "expert", None, None),
    )
    return jax.shard_map(
        shards,
        mesh=mesh,
        in_specs=placed,
        out_specs=P("section", None, "expert", None),
        check_vma=False,
    )
```

profile of v0, /device:TPU:4, one launch (start us, length us, event | category | flops | bytes accessed | tf_op | source)
XLA Modules:
  0.0 1103.9 jit_solution(4250907448235275439)
XLA Ops:
  11.7 1092.3 %while.18 = (s32[]{:T(128)}, bf16[16,2048]{1,0:T(8,128)(2,1)S(1)}, bf16[8,16,2048]{2,1,0:T(8,128)(2,1)}, pred[]{:T(512)}, s32[]{:T(128)}, /*index=5*/bf16[8,16,2...) while((s32[]{:T(128)}, bf16[16,2048]{1,0:T(8,128)(2,1)S(1)}, ...), condition=%wide.region_13.14_spmd.clone, body=%wide.region_0.13_spmd.clone.sunk | while | flops 4300770816 | bytes 111107360 | solution.py:173
  146.8 17.4 %conditional.3 = (bf16[160,2048]{1,0:T(8,128)(2,1)S(1)}, bf16[160]{0:T(256)(128)(2,1)S(1)}) conditional(s32[]{:T(128)} %convert_element_type.182, () %tuple.64, (bf16[32,5,2048]{2,1,0:T(8,128)(2,1)S(1)}, bf16[1024,2048]{1,0:T(8,128)(2,1)}, bf16[32,5,2048]{2,1,0:T(8,128)(2,1)S(1)}, bf16[2048,1024]{1,0:T(8,128)(2,1)}, ...), branch_computations={%region_6.6_spmd, %region_7.8_spmd} | conditional | flops 4031774720 | bytes 93192632 | solution.py:132
  243.4 17.4 %conditional.3 = (bf16[160,2048]{1,0:T(8,128)(2,1)S(1)}, bf16[160]{0:T(256)(128)(2,1)S(1)}) conditional(s32[]{:T(128)} %convert_element_type.182, () %tuple.64, (bf16[32,5,2048]{2,1,0:T(8,128)(2,1)S(1)}, bf16[1024,2048]{1,0:T(8,128)(2,1)}, bf16[32,5,2048]{2,1,0:T(8,128)(2,1)S(1)}, bf16[2048,1024]{1,0:T(8,128)(2,1)}, ...), branch_computations={%region_6.6_spmd, %region_7.8_spmd} | conditional | flops 4031774720 | bytes 93192632 | solution.py:132
  280.2 17.9 %all-to-all-done.2 = bf16[32,5,2048]{2,1,0:T(8,128)(2,1)S(1)} async-done(((bf16[32,5,2048]{2,1,0:T(8,128)(2,1)}), bf16[32,5,2048]{2,1,0:T(8,128)(2,1)S(1)}, u32[]{:S(2)}, u32[]{:S(2)}) %all-to-all-start.2) | async-done | bytes 655392 | tf_op jit(solution)/shard_map/while/body/eval_jaxpr/all_to_all | solution.py:134
  316.2 15.3 %all-to-all-done.1 = bf16[32,5,2048]{2,1,0:T(8,128)(2,1)S(1)} async-done(((bf16[32,5,2048]{2,1,0:T(8,128)(2,1)}), bf16[32,5,2048]{2,1,0:T(8,128)(2,1)S(1)}, u32[]{:S(2)}, u32[]{:S(2)}) %all-to-all-start.1) | async-done | bytes 655392 | tf_op jit(solution)/shard_map/while/body/eval_jaxpr/all_to_all | solution.py:120
  337.3 15.9 %all-to-all-done = bf16[32,5,2048]{2,1,0:T(8,128)(2,1)S(1)} async-done(((bf16[32,5,2048]{2,1,0:T(8,128)(2,1)}), bf16[32,5,2048]{2,1,0:T(8,128)(2,1)S(1)}, u32[]{:S(2)}, u32[]{:S(2)}) %all-to-all-start) | async-done | bytes 655392 | tf_op jit(solution)/shard_map/while/body/eval_jaxpr/all_to_all | solution.py:121
  353.2 17.4 %conditional.3 = (bf16[160,2048]{1,0:T(8,128)(2,1)S(1)}, bf16[160]{0:T(256)(128)(2,1)S(1)}) conditional(s32[]{:T(128)} %convert_element_type.182, () %tuple.64, (bf16[32,5,2048]{2,1,0:T(8,128)(2,1)S(1)}, bf16[1024,2048]{1,0:T(8,128)(2,1)}, bf16[32,5,2048]{2,1,0:T(8,128)(2,1)S(1)}, bf16[2048,1024]{1,0:T(8,128)(2,1)}, ...), branch_computations={%region_6.6_spmd, %region_7.8_spmd} | conditional | flops 4031774720 | bytes 93192632 | solution.py:132
  388.2 14.7 %all-to-all-done.2 = bf16[32,5,2048]{2,1,0:T(8,128)(2,1)S(1)} async-done(((bf16[32,5,2048]{2,1,0:T(8,128)(2,1)}), bf16[32,5,2048]{2,1,0:T(8,128)(2,1)S(1)}, u32[]{:S(2)}, u32[]{:S(2)}) %all-to-all-start.2) | async-done | bytes 655392 | tf_op jit(solution)/shard_map/while/body/eval_jaxpr/all_to_all | solution.py:134
  421.0 15.3 %all-to-all-done.1 = bf16[32,5,2048]{2,1,0:T(8,128)(2,1)S(1)} async-done(((bf16[32,5,2048]{2,1,0:T(8,128)(2,1)}), bf16[32,5,2048]{2,1,0:T(8,128)(2,1)S(1)}, u32[]{:S(2)}, u32[]{:S(2)}) %all-to-all-start.1) | async-done | bytes 655392 | tf_op jit(solution)/shard_map/while/body/eval_jaxpr/all_to_all | solution.py:120
  442.1 15.9 %all-to-all-done = bf16[32,5,2048]{2,1,0:T(8,128)(2,1)S(1)} async-done(((bf16[32,5,2048]{2,1,0:T(8,128)(2,1)}), bf16[32,5,2048]{2,1,0:T(8,128)(2,1)S(1)}, u32[]{:S(2)}, u32[]{:S(2)}) %all-to-all-start) | async-done | bytes 655392 | tf_op jit(solution)/shard_map/while/body/eval_jaxpr/all_to_all | solution.py:121
  458.0 17.4 %conditional.3 = (bf16[160,2048]{1,0:T(8,128)(2,1)S(1)}, bf16[160]{0:T(256)(128)(2,1)S(1)}) conditional(s32[]{:T(128)} %convert_element_type.182, () %tuple.64, (bf16[32,5,2048]{2,1,0:T(8,128)(2,1)S(1)}, bf16[1024,2048]{1,0:T(8,128)(2,1)}, bf16[32,5,2048]{2,1,0:T(8,128)(2,1)S(1)}, bf16[2048,1024]{1,0:T(8,128)(2,1)}, ...), branch_computations={%region_6.6_spmd, %region_7.8_spmd} | conditional | flops 4031774720 | bytes 93192632 | solution.py:132
  493.0 14.7 %all-to-all-done.2 = bf16[32,5,2048]{2,1,0:T(8,128)(2,1)S(1)} async-done(((bf16[32,5,2048]{2,1,0:T(8,128)(2,1)}), bf16[32,5,2048]{2,1,0:T(8,128)(2,1)S(1)}, u32[]{:S(2)}, u32[]{:S(2)}) %all-to-all-start.2) | async-done | bytes 655392 | tf_op jit(solution)/shard_map/while/body/eval_jaxpr/all_to_all | solution.py:134
  525.9 15.3 %all-to-all-done.1 = bf16[32,5,2048]{2,1,0:T(8,128)(2,1)S(1)} async-done(((bf16[32,5,2048]{2,1,0:T(8,128)(2,1)}), bf16[32,5,2048]{2,1,0:T(8,128)(2,1)S(1)}, u32[]{:S(2)}, u32[]{:S(2)}) %all-to-all-start.1) | async-done | bytes 655392 | tf_op jit(solution)/shard_map/while/body/eval_jaxpr/all_to_all | solution.py:120
  547.0 15.9 %all-to-all-done = bf16[32,5,2048]{2,1,0:T(8,128)(2,1)S(1)} async-done(((bf16[32,5,2048]{2,1,0:T(8,128)(2,1)}), bf16[32,5,2048]{2,1,0:T(8,128)(2,1)S(1)}, u32[]{:S(2)}, u32[]{:S(2)}) %all-to-all-start) | async-done | bytes 655392 | tf_op jit(solution)/shard_map/while/body/eval_jaxpr/all_to_all | solution.py:121
  562.9 17.4 %conditional.3 = (bf16[160,2048]{1,0:T(8,128)(2,1)S(1)}, bf16[160]{0:T(256)(128)(2,1)S(1)}) conditional(s32[]{:T(128)} %convert_element_type.182, () %tuple.64, (bf16[32,5,2048]{2,1,0:T(8,128)(2,1)S(1)}, bf16[1024,2048]{1,0:T(8,128)(2,1)}, bf16[32,5,2048]{2,1,0:T(8,128)(2,1)S(1)}, bf16[2048,1024]{1,0:T(8,128)(2,1)}, ...), branch_computations={%region_6.6_spmd, %region_7.8_spmd} | conditional | flops 4031774720 | bytes 93192632 | solution.py:132
  597.9 14.7 %all-to-all-done.2 = bf16[32,5,2048]{2,1,0:T(8,128)(2,1)S(1)} async-done(((bf16[32,5,2048]{2,1,0:T(8,128)(2,1)}), bf16[32,5,2048]{2,1,0:T(8,128)(2,1)S(1)}, u32[]{:S(2)}, u32[]{:S(2)}) %all-to-all-start.2) | async-done | bytes 655392 | tf_op jit(solution)/shard_map/while/body/eval_jaxpr/all_to_all | solution.py:134
  630.7 15.3 %all-to-all-done.1 = bf16[32,5,2048]{2,1,0:T(8,128)(2,1)S(1)} async-done(((bf16[32,5,2048]{2,1,0:T(8,128)(2,1)}), bf16[32,5,2048]{2,1,0:T(8,128)(2,1)S(1)}, u32[]{:S(2)}, u32[]{:S(2)}) %all-to-all-start.1) | async-done | bytes 655392 | tf_op jit(solution)/shard_map/while/body/eval_jaxpr/all_to_all | solution.py:120
  651.8 15.9 %all-to-all-done = bf16[32,5,2048]{2,1,0:T(8,128)(2,1)S(1)} async-done(((bf16[32,5,2048]{2,1,0:T(8,128)(2,1)}), bf16[32,5,2048]{2,1,0:T(8,128)(2,1)S(1)}, u32[]{:S(2)}, u32[]{:S(2)}) %all-to-all-start) | async-done | bytes 655392 | tf_op jit(solution)/shard_map/while/body/eval_jaxpr/all_to_all | solution.py:121
  667.7 17.4 %conditional.3 = (bf16[160,2048]{1,0:T(8,128)(2,1)S(1)}, bf16[160]{0:T(256)(128)(2,1)S(1)}) conditional(s32[]{:T(128)} %convert_element_type.182, () %tuple.64, (bf16[32,5,2048]{2,1,0:T(8,128)(2,1)S(1)}, bf16[1024,2048]{1,0:T(8,128)(2,1)}, bf16[32,5,2048]{2,1,0:T(8,128)(2,1)S(1)}, bf16[2048,1024]{1,0:T(8,128)(2,1)}, ...), branch_computations={%region_6.6_spmd, %region_7.8_spmd} | conditional | flops 4031774720 | bytes 93192632 | solution.py:132
  702.7 14.7 %all-to-all-done.2 = bf16[32,5,2048]{2,1,0:T(8,128)(2,1)S(1)} async-done(((bf16[32,5,2048]{2,1,0:T(8,128)(2,1)}), bf16[32,5,2048]{2,1,0:T(8,128)(2,1)S(1)}, u32[]{:S(2)}, u32[]{:S(2)}) %all-to-all-start.2) | async-done | bytes 655392 | tf_op jit(solution)/shard_map/while/body/eval_jaxpr/all_to_all | solution.py:134
  735.5 15.3 %all-to-all-done.1 = bf16[32,5,2048]{2,1,0:T(8,128)(2,1)S(1)} async-done(((bf16[32,5,2048]{2,1,0:T(8,128)(2,1)}), bf16[32,5,2048]{2,1,0:T(8,128)(2,1)S(1)}, u32[]{:S(2)}, u32[]{:S(2)}) %all-to-all-start.1) | async-done | bytes 655392 | tf_op jit(solution)/shard_map/while/body/eval_jaxpr/all_to_all | solution.py:120
  756.6 15.9 %all-to-all-done = bf16[32,5,2048]{2,1,0:T(8,128)(2,1)S(1)} async-done(((bf16[32,5,2048]{2,1,0:T(8,128)(2,1)}), bf16[32,5,2048]{2,1,0:T(8,128)(2,1)S(1)}, u32[]{:S(2)}, u32[]{:S(2)}) %all-to-all-start) | async-done | bytes 655392 | tf_op jit(solution)/shard_map/while/body/eval_jaxpr/all_to_all | solution.py:121
  772.6 17.4 %conditional.3 = (bf16[160,2048]{1,0:T(8,128)(2,1)S(1)}, bf16[160]{0:T(256)(128)(2,1)S(1)}) conditional(s32[]{:T(128)} %convert_element_type.182, () %tuple.64, (bf16[32,5,2048]{2,1,0:T(8,128)(2,1)S(1)}, bf16[1024,2048]{1,0:T(8,128)(2,1)}, bf16[32,5,2048]{2,1,0:T(8,128)(2,1)S(1)}, bf16[2048,1024]{1,0:T(8,128)(2,1)}, ...), branch_computations={%region_6.6_spmd, %region_7.8_spmd} | conditional | flops 4031774720 | bytes 93192632 | solution.py:132
  840.4 15.3 %all-to-all-done.1 = bf16[32,5,2048]{2,1,0:T(8,128)(2,1)S(1)} async-done(((bf16[32,5,2048]{2,1,0:T(8,128)(2,1)}), bf16[32,5,2048]{2,1,0:T(8,128)(2,1)S(1)}, u32[]{:S(2)}, u32[]{:S(2)}) %all-to-all-start.1) | async-done | bytes 655392 | tf_op jit(solution)/shard_map/while/body/eval_jaxpr/all_to_all | solution.py:120
  861.5 15.9 %all-to-all-done = bf16[32,5,2048]{2,1,0:T(8,128)(2,1)S(1)} async-done(((bf16[32,5,2048]{2,1,0:T(8,128)(2,1)}), bf16[32,5,2048]{2,1,0:T(8,128)(2,1)S(1)}, u32[]{:S(2)}, u32[]{:S(2)}) %all-to-all-start) | async-done | bytes 655392 | tf_op jit(solution)/shard_map/while/body/eval_jaxpr/all_to_all | solution.py:121
  877.4 17.4 %conditional.3 = (bf16[160,2048]{1,0:T(8,128)(2,1)S(1)}, bf16[160]{0:T(256)(128)(2,1)S(1)}) conditional(s32[]{:T(128)} %convert_element_type.182, () %tuple.64, (bf16[32,5,2048]{2,1,0:T(8,128)(2,1)S(1)}, bf16[1024,2048]{1,0:T(8,128)(2,1)}, bf16[32,5,2048]{2,1,0:T(8,128)(2,1)S(1)}, bf16[2048,1024]{1,0:T(8,128)(2,1)}, ...), branch_computations={%region_6.6_spmd, %region_7.8_spmd} | conditional | flops 4031774720 | bytes 93192632 | solution.py:132
  943.2 15.3 %all-to-all-done.1 = bf16[32,5,2048]{2,1,0:T(8,128)(2,1)S(1)} async-done(((bf16[32,5,2048]{2,1,0:T(8,128)(2,1)}), bf16[32,5,2048]{2,1,0:T(8,128)(2,1)S(1)}, u32[]{:S(2)}, u32[]{:S(2)}) %all-to-all-start.1) | async-done | bytes 655392 | tf_op jit(solution)/shard_map/while/body/eval_jaxpr/all_to_all | solution.py:120
  964.4 15.9 %all-to-all-done = bf16[32,5,2048]{2,1,0:T(8,128)(2,1)S(1)} async-done(((bf16[32,5,2048]{2,1,0:T(8,128)(2,1)}), bf16[32,5,2048]{2,1,0:T(8,128)(2,1)S(1)}, u32[]{:S(2)}, u32[]{:S(2)}) %all-to-all-start) | async-done | bytes 655392 | tf_op jit(solution)/shard_map/while/body/eval_jaxpr/all_to_all | solution.py:121
  997.9 14.7 %all-to-all-done.2 = bf16[32,5,2048]{2,1,0:T(8,128)(2,1)S(1)} async-done(((bf16[32,5,2048]{2,1,0:T(8,128)(2,1)}), bf16[32,5,2048]{2,1,0:T(8,128)(2,1)S(1)}, u32[]{:S(2)}, u32[]{:S(2)}) %all-to-all-start.2) | async-done | bytes 655392 | tf_op jit(solution)/shard_map/while/body/eval_jaxpr/all_to_all | solution.py:134
  1030.7 15.3 %all-to-all-done.1 = bf16[32,5,2048]{2,1,0:T(8,128)(2,1)S(1)} async-done(((bf16[32,5,2048]{2,1,0:T(8,128)(2,1)}), bf16[32,5,2048]{2,1,0:T(8,128)(2,1)S(1)}, u32[]{:S(2)}, u32[]{:S(2)}) %all-to-all-start.1) | async-done | bytes 655392 | tf_op jit(solution)/shard_map/while/body/eval_jaxpr/all_to_all | solution.py:120
  1051.8 15.9 %all-to-all-done = bf16[32,5,2048]{2,1,0:T(8,128)(2,1)S(1)} async-done(((bf16[32,5,2048]{2,1,0:T(8,128)(2,1)}), bf16[32,5,2048]{2,1,0:T(8,128)(2,1)S(1)}, u32[]{:S(2)}, u32[]{:S(2)}) %all-to-all-start) | async-done | bytes 655392 | tf_op jit(solution)/shard_map/while/body/eval_jaxpr/all_to_all | solution.py:121
  1085.4 14.7 %all-to-all-done.2 = bf16[32,5,2048]{2,1,0:T(8,128)(2,1)S(1)} async-done(((bf16[32,5,2048]{2,1,0:T(8,128)(2,1)}), bf16[32,5,2048]{2,1,0:T(8,128)(2,1)S(1)}, u32[]{:S(2)}, u32[]{:S(2)}) %all-to-all-start.2) | async-done | bytes 655392 | tf_op jit(solution)/shard_map/while/body/eval_jaxpr/all_to_all | solution.py:134
  (636 shorter events, 746.1 us)
Async XLA Ops:
  11.7 18.4 %collective-permute-start = (bf16[16,2048]{1,0:T(8,128)(2,1)S(1)}, bf16[16,2048]{1,0:T(8,128)(2,1)S(1)}, u32[]{:S(2)}, u32[]{:S(2)}) collective-permute-start(bf16[16,2048]{1,0:T(8,128)(2,1)S(1)} %broadcast_select_fusion.2), channel_id=1, source_target_pairs={{32,0},{64,32},{96,64},{33,1},{65,33},{97,65},{34,2},{66,34},{98,6... | collective-permute-start | bytes 196616 | tf_op jit(solution)/shard_map/while/body/eval_jaxpr/ppermute | solution.py:10
  20.3 25.8 %all-to-all-start.1 = ((bf16[32,5,2048]{2,1,0:T(8,128)(2,1)}), bf16[32,5,2048]{2,1,0:T(8,128)(2,1)S(1)}, u32[]{:S(2)}, u32[]{:S(2)}) async-start(bf16[32,5,2048]{2,1,0:T(8,128)(2,1)} %reshape.261), calls=%async_computation.1 | async-start | bytes 2097152 | tf_op jit(solution)/shard_map/while/body/eval_jaxpr/all_to_all | solution.py:120
  46.1 20.2 %all-to-all-start = ((bf16[32,5,2048]{2,1,0:T(8,128)(2,1)}), bf16[32,5,2048]{2,1,0:T(8,128)(2,1)S(1)}, u32[]{:S(2)}, u32[]{:S(2)}) async-start(bf16[32,5,2048]{2,1,0:T(8,128)(2,1)} %reshape.260), calls=%async_computation | async-start | bytes 2097152 | tf_op jit(solution)/shard_map/while/body/eval_jaxpr/all_to_all | solution.py:121
  100.7 18.0 %collective-permute-start = (bf16[16,2048]{1,0:T(8,128)(2,1)S(1)}, bf16[16,2048]{1,0:T(8,128)(2,1)S(1)}, u32[]{:S(2)}, u32[]{:S(2)}) collective-permute-start(bf16[16,2048]{1,0:T(8,128)(2,1)S(1)} %broadcast_select_fusion.2), channel_id=1, source_target_pairs={{32,0},{64,32},{96,64},{33,1},{65,33},{97,65},{34,2},{66,34},{98,6... | collective-permute-start | bytes 196616 | tf_op jit(solution)/shard_map/while/body/eval_jaxpr/ppermute | solution.py:10
  109.6 19.5 %all-to-all-start.1 = ((bf16[32,5,2048]{2,1,0:T(8,128)(2,1)}), bf16[32,5,2048]{2,1,0:T(8,128)(2,1)S(1)}, u32[]{:S(2)}, u32[]{:S(2)}) async-start(bf16[32,5,2048]{2,1,0:T(8,128)(2,1)} %reshape.261), calls=%async_computation.1 | async-start | bytes 2097152 | tf_op jit(solution)/shard_map/while/body/eval_jaxpr/all_to_all | solution.py:120
  176.9 17.8 %all-to-all-start.2 = ((bf16[32,5,2048]{2,1,0:T(8,128)(2,1)}), bf16[32,5,2048]{2,1,0:T(8,128)(2,1)S(1)}, u32[]{:S(2)}, u32[]{:S(2)}) async-start(bf16[32,5,2048]{2,1,0:T(8,128)(2,1)} %reshape.262), calls=%async_computation.2 | async-start | bytes 2097152 | tf_op jit(solution)/shard_map/while/body/eval_jaxpr/all_to_all | solution.py:134
  205.5 18.1 %all-to-all-start.1 = ((bf16[32,5,2048]{2,1,0:T(8,128)(2,1)}), bf16[32,5,2048]{2,1,0:T(8,128)(2,1)S(1)}, u32[]{:S(2)}, u32[]{:S(2)}) async-start(bf16[32,5,2048]{2,1,0:T(8,128)(2,1)} %reshape.261), calls=%async_computation.1 | async-start | bytes 2097152 | tf_op jit(solution)/shard_map/while/body/eval_jaxpr/all_to_all | solution.py:120
  223.6 19.8 %all-to-all-start = ((bf16[32,5,2048]{2,1,0:T(8,128)(2,1)}), bf16[32,5,2048]{2,1,0:T(8,128)(2,1)S(1)}, u32[]{:S(2)}, u32[]{:S(2)}) async-start(bf16[32,5,2048]{2,1,0:T(8,128)(2,1)} %reshape.260), calls=%async_computation | async-start | bytes 2097152 | tf_op jit(solution)/shard_map/while/body/eval_jaxpr/all_to_all | solution.py:121
  275.3 22.7 %all-to-all-start.2 = ((bf16[32,5,2048]{2,1,0:T(8,128)(2,1)}), bf16[32,5,2048]{2,1,0:T(8,128)(2,1)S(1)}, u32[]{:S(2)}, u32[]{:S(2)}) async-start(bf16[32,5,2048]{2,1,0:T(8,128)(2,1)} %reshape.262), calls=%async_computation.2 | async-start | bytes 2097152 | tf_op jit(solution)/shard_map/while/body/eval_jaxpr/all_to_all | solution.py:134
  308.8 22.7 %all-to-all-start.1 = ((bf16[32,5,2048]{2,1,0:T(8,128)(2,1)}), bf16[32,5,2048]{2,1,0:T(8,128)(2,1)S(1)}, u32[]{:S(2)}, u32[]{:S(2)}) async-start(bf16[32,5,2048]{2,1,0:T(8,128)(2,1)} %reshape.261), calls=%async_computation.1 | async-start | bytes 2097152 | tf_op jit(solution)/shard_map/while/body/eval_jaxpr/all_to_all | solution.py:120
  331.5 21.7 %all-to-all-start = ((bf16[32,5,2048]{2,1,0:T(8,128)(2,1)}), bf16[32,5,2048]{2,1,0:T(8,128)(2,1)S(1)}, u32[]{:S(2)}, u32[]{:S(2)}) async-start(bf16[32,5,2048]{2,1,0:T(8,128)(2,1)} %reshape.260), calls=%async_computation | async-start | bytes 2097152 | tf_op jit(solution)/shard_map/while/body/eval_jaxpr/all_to_all | solution.py:121
  383.3 19.6 %all-to-all-start.2 = ((bf16[32,5,2048]{2,1,0:T(8,128)(2,1)}), bf16[32,5,2048]{2,1,0:T(8,128)(2,1)S(1)}, u32[]{:S(2)}, u32[]{:S(2)}) async-start(bf16[32,5,2048]{2,1,0:T(8,128)(2,1)} %reshape.262), calls=%async_computation.2 | async-start | bytes 2097152 | tf_op jit(solution)/shard_map/while/body/eval_jaxpr/all_to_all | solution.py:134
  413.6 22.7 %all-to-all-start.1 = ((bf16[32,5,2048]{2,1,0:T(8,128)(2,1)}), bf16[32,5,2048]{2,1,0:T(8,128)(2,1)S(1)}, u32[]{:S(2)}, u32[]{:S(2)}) async-start(bf16[32,5,2048]{2,1,0:T(8,128)(2,1)} %reshape.261), calls=%async_computation.1 | async-start | bytes 2097152 | tf_op jit(solution)/shard_map/while/body/eval_jaxpr/all_to_all | solution.py:120
  436.4 21.7 %all-to-all-start = ((bf16[32,5,2048]{2,1,0:T(8,128)(2,1)}), bf16[32,5,2048]{2,1,0:T(8,128)(2,1)S(1)}, u32[]{:S(2)}, u32[]{:S(2)}) async-start(bf16[32,5,2048]{2,1,0:T(8,128)(2,1)} %reshape.260), calls=%async_computation | async-start | bytes 2097152 | tf_op jit(solution)/shard_map/while/body/eval_jaxpr/all_to_all | solution.py:121
  488.1 19.6 %all-to-all-start.2 = ((bf16[32,5,2048]{2,1,0:T(8,128)(2,1)}), bf16[32,5,2048]{2,1,0:T(8,128)(2,1)S(1)}, u32[]{:S(2)}, u32[]{:S(2)}) async-start(bf16[32,5,2048]{2,1,0:T(8,128)(2,1)} %reshape.262), calls=%async_computation.2 | async-start | bytes 2097152 | tf_op jit(solution)/shard_map/while/body/eval_jaxpr/all_to_all | solution.py:134
  518.5 22.7 %all-to-all-start.1 = ((bf16[32,5,2048]{2,1,0:T(8,128)(2,1)}), bf16[32,5,2048]{2,1,0:T(8,128)(2,1)S(1)}, u32[]{:S(2)}, u32[]{:S(2)}) async-start(bf16[32,5,2048]{2,1,0:T(8,128)(2,1)} %reshape.261), calls=%async_computation.1 | async-start | bytes 2097152 | tf_op jit(solution)/shard_map/while/body/eval_jaxpr/all_to_all | solution.py:120
  541.2 21.7 %all-to-all-start = ((bf16[32,5,2048]{2,1,0:T(8,128)(2,1)}), bf16[32,5,2048]{2,1,0:T(8,128)(2,1)S(1)}, u32[]{:S(2)}, u32[]{:S(2)}) async-start(bf16[32,5,2048]{2,1,0:T(8,128)(2,1)} %reshape.260), calls=%async_computation | async-start | bytes 2097152 | tf_op jit(solution)/shard_map/while/body/eval_jaxpr/all_to_all | solution.py:121
  593.0 19.6 %all-to-all-start.2 = ((bf16[32,5,2048]{2,1,0:T(8,128)(2,1)}), bf16[32,5,2048]{2,1,0:T(8,128)(2,1)S(1)}, u32[]{:S(2)}, u32[]{:S(2)}) async-start(bf16[32,5,2048]{2,1,0:T(8,128)(2,1)} %reshape.262), calls=%async_computation.2 | async-start | bytes 2097152 | tf_op jit(solution)/shard_map/while/body/eval_jaxpr/all_to_all | solution.py:134
  623.3 22.7 %all-to-all-start.1 = ((bf16[32,5,2048]{2,1,0:T(8,128)(2,1)}), bf16[32,5,2048]{2,1,0:T(8,128)(2,1)S(1)}, u32[]{:S(2)}, u32[]{:S(2)}) async-start(bf16[32,5,2048]{2,1,0:T(8,128)(2,1)} %reshape.261), calls=%async_computation.1 | async-start | bytes 2097152 | tf_op jit(solution)/shard_map/while/body/eval_jaxpr/all_to_all | solution.py:120
  646.0 21.7 %all-to-all-start = ((bf16[32,5,2048]{2,1,0:T(8,128)(2,1)}), bf16[32,5,2048]{2,1,0:T(8,128)(2,1)S(1)}, u32[]{:S(2)}, u32[]{:S(2)}) async-start(bf16[32,5,2048]{2,1,0:T(8,128)(2,1)} %reshape.260), calls=%async_computation | async-start | bytes 2097152 | tf_op jit(solution)/shard_map/while/body/eval_jaxpr/all_to_all | solution.py:121
  697.8 19.6 %all-to-all-start.2 = ((bf16[32,5,2048]{2,1,0:T(8,128)(2,1)}), bf16[32,5,2048]{2,1,0:T(8,128)(2,1)S(1)}, u32[]{:S(2)}, u32[]{:S(2)}) async-start(bf16[32,5,2048]{2,1,0:T(8,128)(2,1)} %reshape.262), calls=%async_computation.2 | async-start | bytes 2097152 | tf_op jit(solution)/shard_map/while/body/eval_jaxpr/all_to_all | solution.py:134
  728.2 22.7 %all-to-all-start.1 = ((bf16[32,5,2048]{2,1,0:T(8,128)(2,1)}), bf16[32,5,2048]{2,1,0:T(8,128)(2,1)S(1)}, u32[]{:S(2)}, u32[]{:S(2)}) async-start(bf16[32,5,2048]{2,1,0:T(8,128)(2,1)} %reshape.261), calls=%async_computation.1 | async-start | bytes 2097152 | tf_op jit(solution)/shard_map/while/body/eval_jaxpr/all_to_all | solution.py:120
  750.9 21.7 %all-to-all-start = ((bf16[32,5,2048]{2,1,0:T(8,128)(2,1)}), bf16[32,5,2048]{2,1,0:T(8,128)(2,1)S(1)}, u32[]{:S(2)}, u32[]{:S(2)}) async-start(bf16[32,5,2048]{2,1,0:T(8,128)(2,1)} %reshape.260), calls=%async_computation | async-start | bytes 2097152 | tf_op jit(solution)/shard_map/while/body/eval_jaxpr/all_to_all | solution.py:121
  802.6 19.6 %all-to-all-start.2 = ((bf16[32,5,2048]{2,1,0:T(8,128)(2,1)}), bf16[32,5,2048]{2,1,0:T(8,128)(2,1)S(1)}, u32[]{:S(2)}, u32[]{:S(2)}) async-start(bf16[32,5,2048]{2,1,0:T(8,128)(2,1)} %reshape.262), calls=%async_computation.2 | async-start | bytes 2097152 | tf_op jit(solution)/shard_map/while/body/eval_jaxpr/all_to_all | solution.py:134
  833.0 22.7 %all-to-all-start.1 = ((bf16[32,5,2048]{2,1,0:T(8,128)(2,1)}), bf16[32,5,2048]{2,1,0:T(8,128)(2,1)S(1)}, u32[]{:S(2)}, u32[]{:S(2)}) async-start(bf16[32,5,2048]{2,1,0:T(8,128)(2,1)} %reshape.261), calls=%async_computation.1 | async-start | bytes 2097152 | tf_op jit(solution)/shard_map/while/body/eval_jaxpr/all_to_all | solution.py:120
  855.7 21.7 %all-to-all-start = ((bf16[32,5,2048]{2,1,0:T(8,128)(2,1)}), bf16[32,5,2048]{2,1,0:T(8,128)(2,1)S(1)}, u32[]{:S(2)}, u32[]{:S(2)}) async-start(bf16[32,5,2048]{2,1,0:T(8,128)(2,1)} %reshape.260), calls=%async_computation | async-start | bytes 2097152 | tf_op jit(solution)/shard_map/while/body/eval_jaxpr/all_to_all | solution.py:121
  935.9 22.7 %all-to-all-start.1 = ((bf16[32,5,2048]{2,1,0:T(8,128)(2,1)}), bf16[32,5,2048]{2,1,0:T(8,128)(2,1)S(1)}, u32[]{:S(2)}, u32[]{:S(2)}) async-start(bf16[32,5,2048]{2,1,0:T(8,128)(2,1)} %reshape.261), calls=%async_computation.1 | async-start | bytes 2097152 | tf_op jit(solution)/shard_map/while/body/eval_jaxpr/all_to_all | solution.py:120
  958.6 21.7 %all-to-all-start = ((bf16[32,5,2048]{2,1,0:T(8,128)(2,1)}), bf16[32,5,2048]{2,1,0:T(8,128)(2,1)S(1)}, u32[]{:S(2)}, u32[]{:S(2)}) async-start(bf16[32,5,2048]{2,1,0:T(8,128)(2,1)} %reshape.260), calls=%async_computation | async-start | bytes 2097152 | tf_op jit(solution)/shard_map/while/body/eval_jaxpr/all_to_all | solution.py:121
  993.0 19.6 %all-to-all-start.2 = ((bf16[32,5,2048]{2,1,0:T(8,128)(2,1)}), bf16[32,5,2048]{2,1,0:T(8,128)(2,1)S(1)}, u32[]{:S(2)}, u32[]{:S(2)}) async-start(bf16[32,5,2048]{2,1,0:T(8,128)(2,1)} %reshape.262), calls=%async_computation.2 | async-start | bytes 2097152 | tf_op jit(solution)/shard_map/while/body/eval_jaxpr/all_to_all | solution.py:134
  1023.3 22.7 %all-to-all-start.1 = ((bf16[32,5,2048]{2,1,0:T(8,128)(2,1)}), bf16[32,5,2048]{2,1,0:T(8,128)(2,1)S(1)}, u32[]{:S(2)}, u32[]{:S(2)}) async-start(bf16[32,5,2048]{2,1,0:T(8,128)(2,1)} %reshape.261), calls=%async_computation.1 | async-start | bytes 2097152 | tf_op jit(solution)/shard_map/while/body/eval_jaxpr/all_to_all | solution.py:120
  1046.1 21.7 %all-to-all-start = ((bf16[32,5,2048]{2,1,0:T(8,128)(2,1)}), bf16[32,5,2048]{2,1,0:T(8,128)(2,1)S(1)}, u32[]{:S(2)}, u32[]{:S(2)}) async-start(bf16[32,5,2048]{2,1,0:T(8,128)(2,1)} %reshape.260), calls=%async_computation | async-start | bytes 2097152 | tf_op jit(solution)/shard_map/while/body/eval_jaxpr/all_to_all | solution.py:121
  1080.5 19.6 %all-to-all-start.2 = ((bf16[32,5,2048]{2,1,0:T(8,128)(2,1)}), bf16[32,5,2048]{2,1,0:T(8,128)(2,1)S(1)}, u32[]{:S(2)}, u32[]{:S(2)}) async-start(bf16[32,5,2048]{2,1,0:T(8,128)(2,1)} %reshape.262), calls=%async_computation.2 | async-start | bytes 2097152 | tf_op jit(solution)/shard_map/while/body/eval_jaxpr/all_to_all | solution.py:134
  (55 other events, 394.6 us)
where the time goes:
time: 1110 us; the launch traced here: 1100 us
  waiting for transfers between devices  557 us (50%)
  starting transfers between devices  206 us (19%)
  matrix products  158 us (14%)
  local copies, waits for them, and re-layouts  105 us (9%)
  other arithmetic  66.6 us (6%)
    all_to_all x11, waiting for transfers between devices, advance(): lax.all_to_all(sent_grad, 'expert', split_axis=0, concat_axis=0, tiled=True)  168 us
    all_to_all x11, waiting for transfers between devices, advance(): lax.all_to_all(returned.reshape(experts, capacity, width), 'expert', spli...  159 us
    all_to_all x11, waiting for transfers between devices, advance(): lax.all_to_all(sent_normed, 'expert', split_axis=0, concat_axis=0, tiled=...  155 us
    all_to_all x11, waiting for transfers between devices, advance(): lax.all_to_all(dprob.reshape(experts, capacity).astype(jnp.bfloat16), 'ex...  73.6 us
    all_to_all x11, starting transfers between devices, advance(): lax.all_to_all(sent_normed, 'expert', split_axis=0, concat_axis=0, tiled=...  50.2 us
    all_to_all x11, starting transfers between devices, advance(): lax.all_to_all(dprob.reshape(experts, capacity).astype(jnp.bfloat16), 'ex...  44.1 us
    all_to_all x11, starting transfers between devices, advance(): lax.all_to_all(sent_grad, 'expert', split_axis=0, concat_axis=0, tiled=True)  43.3 us
    all_to_all x11, starting transfers between devices, advance(): lax.all_to_all(returned.reshape(experts, capacity, width), 'expert', spli...  43.2 us
  transfers between devices with their start and end apart: 55, of which 45 were waited for; matrix products, arithmetic and copies ran while one was open for 12% of the time, Pallas kernels for 0%

commit v1 on v0

v1 whole, which is shorter than its diff:
```python
import jax
import jax.numpy as jnp
from jax import lax
from jax.experimental import pallas as pl
from jax.experimental.pallas import tpu as pltpu
from jax.sharding import PartitionSpec as P

MICRO = 8
TOK = 16
MOST = 5
BLOCKS = 8
LINE = 4
SECTIONS = 4
EXPERTS = 32
GATHERED = BLOCKS * TOK
GROUP = 48
SLOTS = LINE * GROUP
LANES = 128
CONTRACT_LAST = (((1,), (1,)), ((), ()))


def kernel(
    x_ref,
    top_ref,
    sel_ref,
    selt_ref,
    gain_ref,
    router_ref,
    wg_ref,
    wu_ref,
    wd_ref,
    out_ref,
    wcat,
    wdown,
    xn,
    xg,
    dg,
    xr,
    dr,
    rr,
    xs,
    ds,
    cs,
    es,
    ap,
    ac,
    hd,
    pm,
    dcat,
    w_sem,
    xg_s,
    xg_r,
    xr_s,
    xr_r,
    dg_s,
    dg_r,
    dr_s,
    dr_r,
    c_s,
    c_r,
    rr_s,
    rr_r,
    tg_s,
):
    width = x_ref.shape[2]
    inner = wd_ref.shape[0]
    section = lax.axis_index("section")
    me = lax.axis_index("expert")
    z = me // 8
    y = (me // 2) % 4
    x = me % 2
    last = SECTIONS - 1

    def place(k):
        odd = k % 2
        g = z * (1 - odd) + y * odd
        h = y * (1 - odd) + z * odd
        return g, h, 8 - 6 * odd, 2 + 6 * odd

    def rows(start, size):
        return pl.ds(pl.multiple_of(start, 16), size)

    def block_target(k, b):
        _, h, gs, hs = place(k)
        return (b // 2) * gs + h * hs + b % 2

    def my_block(k):
        g, _, _, _ = place(k)
        return g * 2 + x

    def remote(src, dst, ssem, rsem, sec, dev):
        pltpu.make_async_remote_copy(
            src_ref=src,
            dst_ref=dst,
            send_sem=ssem,
            recv_sem=rsem,
            device_id={"section": sec, "expert": dev},
            device_id_type=pl.DeviceIdType.MESH,
        ).start()

    def wait_bytes(ref, sem):
        pltpu.make_async_copy(ref, ref, sem).wait()

    def spread_out(src, k, sec, ssem):
        mine = my_block(k)

        @pl.loop(0, BLOCKS)
        def _(j):
            b = (mine + j) % BLOCKS
            remote(src, dg.at[k, rows(mine * TOK, TOK)], ssem, dg_r.at[k], sec, block_target(k, b))

    def spread_in(src, dst, k, ssem, rsem):
        mine = my_block(k)
        pltpu.make_async_copy(src, dst.at[k, rows(mine * TOK, TOK)], rsem).start()

        @pl.loop(1, BLOCKS)
        def _(j):
            b = (mine + j) % BLOCKS
            remote(src, dst.at[k, rows(mine * TOK, TOK)], ssem, rsem, section, block_target(k, b))

    def along_line(stage, dst, k, ssem, rsem):
        g, h, gs, hs = place(k)
        slot = k % 2
        to = dst.at[k, rows(h * GROUP, GROUP)]
        pltpu.make_async_copy(stage.at[slot, rows(h * GROUP, GROUP)], to, rsem).start()

        @pl.loop(1, LINE)
        def _(j):
            d = (h + j) % LINE
            remote(
                stage.at[slot, rows(d * GROUP, GROUP)], to, ssem, rsem, section, g * gs + d * hs + x
            )

    def pack(src, stage, k):
        slot = k % 2

        @pl.loop(0, width // 512)
        def _(n):
            cols = pl.ds(pl.multiple_of(n * 512, 512), 512)
            stage[slot, :, cols] = jnp.dot(
                sel_ref[k], src[k, :, cols], preferred_element_type=jnp.float32
            ).astype(jnp.bfloat16)

    def inverse_of(xf):
        return lax.rsqrt(jnp.mean(xf * xf, axis=-1, keepdims=True) + 1e-05)

    def send_normed(k):
        xf = x_ref[k].astype(jnp.float32)
        xn[k] = (xf * inverse_of(xf) * gain_ref[...]).astype(jnp.bfloat16)
        spread_in(xn.at[k], xg, k, xg_s.at[k], xg_r.at[k])

    def pack_normed(k):
        wait_bytes(xg.at[k], xg_r.at[k])

        @pl.when(k >= 2)
        def _():
            wait_bytes(xs.at[0, pl.ds(0, SLOTS - GROUP)], xr_s.at[k - 2])

        pack(xg, xs, k)
        along_line(xs, xr, k, xr_s.at[k], xr_r.at[k])

    def forward(k):
        wait_bytes(xr.at[k], xr_r.at[k])
        logits = jnp.dot(
            xr[k], wcat[:, pl.ds(2 * inner, LANES)], preferred_element_type=jnp.float32
        )
        lane = lax.broadcasted_iota(jnp.int32, (SLOTS, LANES), 1)
        raised = jnp.where(lane < EXPERTS, jnp.exp(logits), 0.0)
        probs = raised / jnp.sum(raised, axis=-1, keepdims=True)
        pm[k] = probs
        picked = jnp.sum(jnp.where(lane == me, probs, 0.0), axis=-1, keepdims=True)

        @pl.loop(0, inner // 256)
        def _(n):
            cols = pl.ds(pl.multiple_of(n * 256, 256), 256)
            more = pl.ds(pl.multiple_of(inner + n * 256, 256), 256)
            gate = jnp.dot(xr[k], wcat[:, cols], preferred_element_type=jnp.float32)
            up = jnp.dot(xr[k], wcat[:, more], preferred_element_type=jnp.float32)
            squash = jax.nn.sigmoid(gate)
            active = gate * squash
            hd[k, :, cols] = (active * up).astype(jnp.bfloat16)
            ac[k, :, cols] = (picked * active).astype(jnp.bfloat16)
            ap[k, :, cols] = (picked * up * squash * (1.0 + gate * (1.0 - squash))).astype(
                jnp.bfloat16
            )

    def normed_step(i):
        @pl.when(i < MICRO)
        def _():
            pack_normed(i)

        @pl.when(jnp.logical_and(i >= 1, i <= MICRO))
        def _():
            forward(i - 1)

    def pack_grad(k):
        wait_bytes(dg.at[k], dg_r.at[k])

        @pl.when(k >= 2)
        def _():
            wait_bytes(ds.at[0, pl.ds(0, SLOTS - GROUP)], dr_s.at[k - 2])

        pack(dg, ds, k)
        along_line(ds, dr, k, dr_s.at[k], dr_r.at[k])

    def backward(k):
        wait_bytes(dr.at[k], dr_r.at[k])
        slot = k % 2

        def part(n, dprob):
            cols = pl.ds(pl.multiple_of(n * 256, 256), 256)
            more = pl.ds(pl.multiple_of(inner + n * 256, 256), 256)
            dh = lax.dot_general(
                dr[k], wdown[cols, :], CONTRACT_LAST, preferred_element_type=jnp.float32
            )
            dcat[:, cols] = (dh * ap[k, :, cols].astype(jnp.float32)).astype(jnp.bfloat16)
            dcat[:, more] = (dh * ac[k, :, cols].astype(jnp.float32)).astype(jnp.bfloat16)
            return dprob + jnp.sum(
                dh * hd[k, :, cols].astype(jnp.float32), axis=-1, keepdims=True
            )

        dprob = lax.fori_loop(0, inner // 256, part, jnp.zeros((SLOTS, 1), jnp.float32))
        lane = lax.broadcasted_iota(jnp.int32, (SLOTS, LANES), 1)
        probs = pm[k]
        own = jnp.where(lane == me, 1.0, 0.0)
        picked = jnp.sum(probs * own, axis=-1, keepdims=True)
        dcat[:, pl.ds(2 * inner, LANES)] = (picked * dprob * (own - probs)).astype(jnp.bfloat16)

        @pl.when(k >= 2)
        def _():
            wait_bytes(cs.at[0, pl.ds(0, SLOTS - GROUP)], c_s.at[k - 2])

        @pl.loop(0, width // 256)
        def _(n):
            cols = pl.ds(pl.multiple_of(n * 256, 256), 256)
            cs[slot, :, cols] = lax.dot_general(
                dcat[...], wcat[cols, :], CONTRACT_LAST, preferred_element_type=jnp.float32
            ).astype(jnp.bfloat16)

        along_line(cs, xr, k, c_s.at[k], c_r.at[k])

    def unpack(k):
        wait_bytes(xr.at[k], c_r.at[k])
        slot = k % 2

        @pl.when(k >= 2)
        def _():
            wait_bytes(es.at[0, pl.ds(0, GATHERED - TOK)], rr_s.at[k - 2])

        @pl.loop(0, width // 512)
        def _(n):
            cols = pl.ds(pl.multiple_of(n * 512, 512), 512)
            es[slot, :, cols] = jnp.dot(
                selt_ref[k], xr[k, :, cols], preferred_element_type=jnp.float32
            ).astype(jnp.bfloat16)

        mine = my_block(k)
        to = rr.at[k, rows(mine * TOK, TOK)]
        pltpu.make_async_copy(es.at[slot, rows(mine * TOK, TOK)], to, rr_r.at[k]).start()

        @pl.loop(1, BLOCKS)
        def _(j):
            b = (mine + j) % BLOCKS
            remote(
                es.at[slot, rows(b * TOK, TOK)],
                to,
                rr_s.at[k],
                rr_r.at[k],
                section,
                block_target(k, b),
            )

    def finish(k):
        wait_bytes(rr.at[k], rr_r.at[k])
        dxn = rr[k, pl.ds(0, TOK)].astype(jnp.float32)
        for b in range(1, BLOCKS):
            dxn = dxn + rr[k, pl.ds(b * TOK, TOK)].astype(jnp.float32)
        xf = x_ref[k].astype(jnp.float32)
        inv = inverse_of(xf)
        scaled = gain_ref[...] * dxn
        mean = jnp.mean(xf * scaled, axis=-1, keepdims=True)
        grad = dg[k, rows(my_block(k) * TOK, TOK)].astype(jnp.float32)
        out_ref[k] = (grad + inv * scaled - xf * (inv * inv * inv * mean)).astype(jnp.bfloat16)

        @pl.when(section > 0)
        def _():
            spread_out(out_ref.at[k], k, section - 1, dg_s.at[k])

    weights = [
        pltpu.make_async_copy(wg_ref, wcat.at[:, pl.ds(0, inner)], w_sem.at[0]),
        pltpu.make_async_copy(wu_ref, wcat.at[:, pl.ds(inner, inner)], w_sem.at[1]),
        pltpu.make_async_copy(router_ref, wcat.at[:, pl.ds(2 * inner, LANES)], w_sem.at[2]),
        pltpu.make_async_copy(wd_ref, wdown, w_sem.at[3]),
    ]
    for copy in weights:
        copy.start()

    for half in range(2):
        k = section * 2 + half

        @pl.when(section == last)
        def _():
            spread_in(top_ref.at[half], dg, k, tg_s.at[half], dg_r.at[k])

        @pl.when(section < last)
        def _():
            spread_out(top_ref.at[half], k, last, tg_s.at[half])

    @pl.loop(0, MICRO)
    def _(k):
        send_normed(k)

    for copy in weights:
        copy.wait()

    ahead = jnp.where(section == last, AHEAD_LAST, MICRO)

    @pl.loop(0, ahead + 1)
    def _(i):
        normed_step(i)

    @pl.loop(0, MICRO + 1)
    def _(k):
        @pl.when(k < MICRO)
        def _():
            pack_grad(k)

        @pl.when(k >= 1)
        def _():
            unpack(k - 1)

        normed_step(k + ahead + 1)

        @pl.when(k < MICRO)
        def _():
            backward(k)

        @pl.when(k >= 1)
        def _():
            finish(k - 1)

    @pl.loop(MICRO - 2, MICRO)
    def _(k):
        line = pl.ds(0, SLOTS - GROUP)
        wait_bytes(xs.at[0, line], xr_s.at[k])
        wait_bytes(ds.at[0, line], dr_s.at[k])
        wait_bytes(cs.at[0, line], c_s.at[k])
        wait_bytes(es.at[0, pl.ds(0, GATHERED - TOK)], rr_s.at[k])

    @pl.loop(0, MICRO)
    def _(k):
        wait_bytes(xg.at[0, pl.ds(0, GATHERED - TOK)], xg_s.at[k])

        @pl.when(section > 0)
        def _():
            wait_bytes(dg.at[0], dg_s.at[k])

    for half in range(2):

        @pl.when(section == last)
        def _():
            wait_bytes(dg.at[0, pl.ds(0, GATHERED - TOK)], tg_s.at[half])

        @pl.when(section < last)
        def _():
            wait_bytes(dg.at[0], tg_s.at[half])


AHEAD_LAST = 2


def selections(ids):
    gathered = lax.all_gather(ids, "expert", axis=0).reshape(4, 4, 2, MICRO // 2, 2, TOK, 8)
    me = lax.axis_index("expert")
    z, y, x = me // 8, (me // 2) % 4, me % 2
    even = lax.dynamic_index_in_dim(gathered[:, :, :, :, 0], y, 1, False)
    odd = lax.dynamic_index_in_dim(gathered[:, :, :, :, 1], z, 0, False)
    blocks = jnp.stack([even, odd], axis=3).reshape(BLOCKS, MICRO, TOK, 8)
    blocks = jnp.transpose(blocks, (1, 0, 2, 3))
    line = jnp.arange(LINE, dtype=jnp.int32)
    expert = jnp.stack([z * 8 + line * 2 + x, line * 8 + y * 2 + x])
    expert = jnp.tile(expert, (MICRO // 2, 1))
    named = jnp.any(blocks[:, None] == expert[:, :, None, None, None], axis=-1)
    before = jnp.arange(TOK)[None, :] < jnp.arange(TOK)[:, None]
    rank = jnp.sum((named[:, :, :, None, :] & before).astype(jnp.int32), axis=-1)
    slot = jnp.where(named, rank + MOST * jnp.arange(BLOCKS, dtype=jnp.int32)[:, None], -1)
    slot = slot.reshape(MICRO, LINE, GATHERED)
    group = jnp.arange(GROUP, dtype=jnp.int32)
    sel = (slot[:, :, None, :] == group[:, None]).astype(jnp.bfloat16)
    selt = (jnp.transpose(slot, (0, 2, 1))[..., None] == group).astype(jnp.bfloat16)
    return sel.reshape(MICRO, SLOTS, GATHERED), selt.reshape(MICRO, GATHERED, SLOTS)


def shards(layer_inputs, top_grad, expert_ids, router, norm_gain, w_gate, w_up, w_down):
    width = layer_inputs.shape[3]
    inner = w_down.shape[2]
    sel, selt = selections(expert_ids[0])
    padded = jnp.pad(router[0], ((0, 0), (0, LANES - EXPERTS)))
    vmem = pl.BlockSpec(memory_space=pltpu.VMEM)
    hbm = pl.BlockSpec(memory_space=pl.ANY)
    half = jnp.bfloat16
    line = (MICRO, SLOTS, width)
    gather = (MICRO, GATHERED, width)
    factor = (MICRO, SLOTS, inner)
    dma = pltpu.SemaphoreType.DMA
    out = pl.pallas_call(
        kernel,
        out_shape=jax.ShapeDtypeStruct((MICRO, TOK, width), half),
        in_specs=[vmem] * 5 + [hbm] * 4,
        out_specs=vmem,
        scratch_shapes=[
            pltpu.VMEM((width, 2 * inner + LANES), half),
            pltpu.VMEM((inner, width), half),
            pltpu.VMEM((MICRO, TOK, width), half),
            pltpu.VMEM(gather, half),
            pltpu.VMEM(gather, half),
            pltpu.VMEM(line, half),
            pltpu.VMEM(line, half),
            pltpu.VMEM(gather, half),
            pltpu.VMEM((2, SLOTS, width), half),
            pltpu.VMEM((2, SLOTS, width), half),
            pltpu.VMEM((2, SLOTS, width), half),
            pltpu.VMEM((2, GATHERED, width), half),
            pltpu.VMEM(factor, half),
            pltpu.VMEM(factor, half),
            pltpu.VMEM(factor, half),
            pltpu.VMEM((MICRO, SLOTS, LANES), jnp.float32),
            pltpu.VMEM((SLOTS, 2 * inner + LANES), half),
            dma((4,)),
        ]
        + [dma((MICRO,)) for _ in range(12)]
        + [dma((2,))],
        compiler_params=pltpu.CompilerParams(
            has_side_effects=True, vmem_limit_bytes=60 * 1024 * 1024
        ),
    )(
        layer_inputs[0],
        top_grad,
        sel,
        selt,
        norm_gain.astype(jnp.float32),
        padded,
        w_gate[0, 0],
        w_up[0, 0],
        w_down[0, 0],
    )
    return out[None]


def solution(mesh):
    placed = (
        P("section", None, "expert", None),
        P("section", "expert", None),
        P("section", None, "expert", None),
        P("section", None, None),
        P("section", None),
        P("section", "expert", None, None),
        P("section", "expert", None, None),
        P("section", "expert", None, None),
    )
    return jax.shard_map(
        shards,
        mesh=mesh,
        in_specs=placed,
        out_specs=P("section", None, "expert", None),
        check_vma=False,
    )
```

time: 1110 us -> 501 us (0.45)
  the two profiles are of different devices: /device:TPU:4 before, /device:TPU:0 now
where the time goes in v1:
time: 501 us; the launch traced here: 500 us
  Pallas kernels  396 us (79%)
  blocking collectives  92.8 us (19%)
  other arithmetic  7.26 us (1%)
    pallas_call x1, Pallas kernels, shards(): pl.pallas_call(kernel, out_shape=jax.ShapeDtypeStruct((MICRO, TOK, width)...  396 us
    all_gather x1, blocking collectives, selections(): lax.all_gather(ids, 'expert', axis=0)  92.8 us

profile of v1, /device:TPU:0, one launch (start us, length us, event | category | flops | bytes accessed | tf_op | source)
XLA Modules:
  0.0 500.3 jit_solution(6212624452588499954)
XLA Ops:
  0.0 92.8 %all_gather.3 = s32[32,8,16,8]{2,3,1,0:T(8,128)S(1)} all-gather(s32[1,8,16,8]{2,3,1,0:T(8,128)} %param.10), channel_id=1, replica_groups=mesh['section'=4,'expert'=32] {'expert'}, dimensions={0}, use_global_device_ids=true | all-gather | bytes 135168 | tf_op jit(solution)/shard_map/all_gather | solution.py:373
  92.8 0.0 copy-start
  92.8 0.1 fusion.1
  92.9 0.0 copy-start.1
  93.1 0.4 compare_reduce_fusion
  93.5 4.4 convert_reduce_fusion
  97.9 0.1 reduce_sum.12
  98.0 0.1 reduce_or.12
  98.1 0.1 add.97
  98.2 0.1 add.98
  98.3 0.1 eq.65
  98.4 0.3 copy.31
  98.7 0.1 eq.62
  98.8 0.9 compare_convert_fusion.selt_ref
  99.7 0.9 fusion.sel_ref
  100.6 0.0 copy-done
  100.6 0.3 copy.33
  100.8 0.9 pad.4.router_ref
  101.7 0.0 copy-done.1
  101.7 0.6 convert_element_type.19.gain_ref
  102.3 396.1 %shard_map.82 = bf16[8,16,2048]{2,1,0:T(8,128)(2,1)} custom-call(bf16[8,16,2048]{2,1,0:T(8,128)(2,1)} %bitcast.38, bf16[2,16,2048]{2,1,0:T(8,128)(2,1)} %top_ref.1, bf16[8,192,128]{2,1,0:T(8,128)(2,1)} %fusion.sel_ref, bf16[8,128,192]{2,1,0:T(8,128)(2,1)} %compare_convert_fusion.selt_ref, f32[1,2048]{1,0:T(1,128)} %convert_element_type.19.gain_ref, ...), custom_call_target="tpu_custom_call" | custom-call | tf_op jit(solution)/shard_map/pallas_call | solution.py:406
  498.5 1.9 copy.41
  (10 shorter events, 0.1 us)
Async XLA Ops:
  92.8 7.8 %copy-start = (bf16[1,2048,32]{1,2,0:T(8,128)(2,1)S(1)}, bf16[1,2048,32]{1,2,0:T(8,128)(2,1)}, u32[]{:S(2)}) copy-start(bf16[1,2048,32]{1,2,0:T(8,128)(2,1)} %param.11) | copy-start | bytes 393220
  92.9 8.9 %copy-start.1 = (bf16[1,2048]{1,0:T(2,128)(2,1)S(1)}, bf16[1,2048]{1,0:T(2,128)(2,1)}, u32[]{:S(2)}) copy-start(bf16[1,2048]{1,0:T(2,128)(2,1)} %param.12) | copy-start | bytes 12292

commit v2 on v1

--- a/solution.py
+++ b/solution.py
@@ -22,8 +22,7 @@
 def kernel(
     x_ref,
     top_ref,
-    sel_ref,
-    selt_ref,
+    ids_ref,
     gain_ref,
     router_ref,
     wg_ref,
@@ -47,6 +46,8 @@
     hd,
     pm,
     dcat,
+    sel_ref,
+    selt_ref,
     w_sem,
     xg_s,
     xg_r,
@@ -141,12 +142,41 @@
                 sel_ref[k], src[k, :, cols], preferred_element_type=jnp.float32
             ).astype(jnp.bfloat16)
 
+    def select(k):
+        g, h, gs, hs = place(k)
+        named = xg[k, :, pl.ds(width, LANES)]
+        here = lax.broadcasted_iota(jnp.int32, (GATHERED, GATHERED), 0)
+        other = lax.broadcasted_iota(jnp.int32, (GATHERED, GATHERED), 1)
+        before = jnp.logical_and(here // TOK == other // TOK, other < here)
+        rank = jnp.dot(
+            before.astype(jnp.float32).astype(jnp.bfloat16), named, preferred_element_type=jnp.float32
+        )
+        block = lax.broadcasted_iota(jnp.int32, (GATHERED, LANES), 0) // TOK
+        code = rank + (MOST * block + 1).astype(jnp.float32)
+        code = (named.astype(jnp.float32) * code).astype(jnp.bfloat16)
+        row = lax.broadcasted_iota(jnp.int32, (SLOTS, LANES), 0)
+        lane = lax.broadcasted_iota(jnp.int32, (SLOTS, LANES), 1)
+        expert = g * gs + (row // GROUP) * hs + x
+        pick = (lane == expert).astype(jnp.float32).astype(jnp.bfloat16)
+        held = lax.dot_general(pick, code, CONTRACT_LAST, preferred_element_type=jnp.float32)
+        want = (row % GROUP + 1).astype(jnp.float32)
+        sel_ref[k] = (held == want).astype(jnp.float32).astype(jnp.bfloat16)
+        held = lax.dot_general(code, pick, CONTRACT_LAST, preferred_element_type=jnp.float32)
+        want = lax.broadcasted_iota(jnp.int32, (GATHERED, SLOTS), 1) % GROUP + 1
+        selt_ref[k] = (held == want.astype(jnp.float32)).astype(jnp.float32).astype(jnp.bfloat16)
+
     def inverse_of(xf):
         return lax.rsqrt(jnp.mean(xf * xf, axis=-1, keepdims=True) + 1e-05)
 
     def send_normed(k):
         xf = x_ref[k].astype(jnp.float32)
-        xn[k] = (xf * inverse_of(xf) * gain_ref[...]).astype(jnp.bfloat16)
+        xn[k, :, pl.ds(0, width)] = (xf * inverse_of(xf) * gain_ref[...]).astype(jnp.bfloat16)
+        ids = ids_ref[k]
+        lane = lax.broadcasted_iota(jnp.int32, (TOK, LANES), 1)
+        named = jnp.zeros((TOK, LANES), jnp.float32)
+        for choice in range(ids.shape[1]):
+            named = jnp.where(ids[:, choice : choice + 1] == lane, 1.0, named)
+        xn[k, :, pl.ds(width, LANES)] = named.astype(jnp.bfloat16)
         spread_in(xn.at[k], xg, k, xg_s.at[k], xg_r.at[k])
 
     def pack_normed(k):
@@ -156,6 +186,7 @@
         def _():
             wait_bytes(xs.at[0, pl.ds(0, SLOTS - GROUP)], xr_s.at[k - 2])
 
+        select(k)
         pack(xg, xs, k)
         along_line(xs, xr, k, xr_s.at[k], xr_r.at[k])
 
@@ -369,32 +400,9 @@
 AHEAD_LAST = 2
 
 
-def selections(ids):
-    gathered = lax.all_gather(ids, "expert", axis=0).reshape(4, 4, 2, MICRO // 2, 2, TOK, 8)
-    me = lax.axis_index("expert")
-    z, y, x = me // 8, (me // 2) % 4, me % 2
-    even = lax.dynamic_index_in_dim(gathered[:, :, :, :, 0], y, 1, False)
-    odd = lax.dynamic_index_in_dim(gathered[:, :, :, :, 1], z, 0, False)
-    blocks = jnp.stack([even, odd], axis=3).reshape(BLOCKS, MICRO, TOK, 8)
-    blocks = jnp.transpose(blocks, (1, 0, 2, 3))
-    line = jnp.arange(LINE, dtype=jnp.int32)
-    expert = jnp.stack([z * 8 + line * 2 + x, line * 8 + y * 2 + x])
-    expert = jnp.tile(expert, (MICRO // 2, 1))
-    named = jnp.any(blocks[:, None] == expert[:, :, None, None, None], axis=-1)
-    before = jnp.arange(TOK)[None, :] < jnp.arange(TOK)[:, None]
-    rank = jnp.sum((named[:, :, :, None, :] & before).astype(jnp.int32), axis=-1)
-    slot = jnp.where(named, rank + MOST * jnp.arange(BLOCKS, dtype=jnp.int32)[:, None], -1)
-    slot = slot.reshape(MICRO, LINE, GATHERED)
-    group = jnp.arange(GROUP, dtype=jnp.int32)
-    sel = (slot[:, :, None, :] == group[:, None]).astype(jnp.bfloat16)
-    selt = (jnp.transpose(slot, (0, 2, 1))[..., None] == group).astype(jnp.bfloat16)
-    return sel.reshape(MICRO, SLOTS, GATHERED), selt.reshape(MICRO, GATHERED, SLOTS)
-
-
 def shards(layer_inputs, top_grad, expert_ids, router, norm_gain, w_gate, w_up, w_down):
     width = layer_inputs.shape[3]
     inner = w_down.shape[2]
-    sel, selt = selections(expert_ids[0])
     padded = jnp.pad(router[0], ((0, 0), (0, LANES - EXPERTS)))
     vmem = pl.BlockSpec(memory_space=pltpu.VMEM)
     hbm = pl.BlockSpec(memory_space=pl.ANY)
@@ -406,13 +414,13 @@
     out = pl.pallas_call(
         kernel,
         out_shape=jax.ShapeDtypeStruct((MICRO, TOK, width), half),
-        in_specs=[vmem] * 5 + [hbm] * 4,
+        in_specs=[vmem] * 4 + [hbm] * 4,
         out_specs=vmem,
         scratch_shapes=[
             pltpu.VMEM((width, 2 * inner + LANES), half),
             pltpu.VMEM((inner, width), half),
-            pltpu.VMEM((MICRO, TOK, width), half),
-            pltpu.VMEM(gather, half),
+            pltpu.VMEM((MICRO, TOK, width + LANES), half),
+            pltpu.VMEM((MICRO, GATHERED, width + LANES), half),
             pltpu.VMEM(gather, half),
             pltpu.VMEM(line, half),
             pltpu.VMEM(line, half),
@@ -426,6 +434,8 @@
             pltpu.VMEM(factor, half),
             pltpu.VMEM((MICRO, SLOTS, LANES), jnp.float32),
             pltpu.VMEM((SLOTS, 2 * inner + LANES), half),
+            pltpu.VMEM((MICRO, SLOTS, GATHERED), half),
+            pltpu.VMEM((MICRO, GATHERED, SLOTS), half),
             dma((4,)),
         ]
         + [dma((MICRO,)) for _ in range(12)]
@@ -436,8 +446,7 @@
     )(
         layer_inputs[0],
         top_grad,
-        sel,
-        selt,
+        expert_ids[0],
         norm_gain.astype(jnp.float32),
         padded,
         w_gate[0, 0],

time: 501 us -> 414 us (0.83)
  blocking collectives: 92.8 us -> 0 us
  Pallas kernels: 396 us -> 407 us
  other arithmetic: 7.26 us -> 1.3 us
    all_gather x1 -> x0, blocking collectives: 92.8 us -> none  [selections(): lax.all_gather(ids, 'expert', axis=0)]
    pallas_call x1, Pallas kernels: 396 us -> 407 us  [shards(): pl.pallas_call(kernel, out_shape=jax.ShapeDtypeStruct((MICRO, TOK, width)...]
where the time goes in v2:
time: 414 us
  Pallas kernels  407 us (98%)
  local copies, waits for them, and re-layouts  5.42 us (1%)
    pallas_call x1, Pallas kernels, shards(): pl.pallas_call(kernel, out_shape=jax.ShapeDtypeStruct((MICRO, TOK, width)...  407 us

profile of v2, /device:TPU:0, one launch (start us, length us, event | category | flops | bytes accessed | tf_op | source)
XLA Modules:
  0.0 414.2 jit_solution(2609070242273292249)
XLA Ops:
  0.0 1.3 convert_element_type.5.gain_ref
  1.3 1.5 copy.9
  2.8 1.2 copy.10
  3.9 0.9 pad.4.router_ref
  4.8 407.4 %shard_map.82 = bf16[8,16,2048]{2,1,0:T(8,128)(2,1)} custom-call(bf16[8,16,2048]{2,1,0:T(8,128)(2,1)} %bitcast.12, bf16[2,16,2048]{2,1,0:T(8,128)(2,1)} %top_ref.1, s32[8,16,8]{2,1,0:T(8,128)} %bitcast.13, f32[1,2048]{1,0:T(1,128)} %convert_element_type.5.gain_ref, bf16[2048,128]{1,0:T(8,128)(2,1)} %pad.4.router_ref, bf16[2048,1024]{1,0:T(8,128)(2,1)} %bitcast.7, ...), custom_call_target="tpu_custom_call" | custom-call | tf_op jit(solution)/shard_map/pallas_call | solution.py:414
  412.3 1.9 copy.12

commit v3 on v2

v3 whole, which is shorter than its diff:
```python
import jax
import jax.numpy as jnp
from jax import lax
from jax.experimental import pallas as pl
from jax.experimental.pallas import tpu as pltpu
from jax.sharding import PartitionSpec as P

MICRO = 8
TOK = 16
MOST = 5
SECTIONS = 4
EXPERTS = 32
LANES = 128
TILE = 16
SLOTS = EXPERTS * MOST
PART = MOST * TILE
ROWS = SLOTS * TILE
OWN = TOK * TILE
AHEAD_LAST = 2
CONTRACT_LAST = (((1,), (1,)), ((), ()))


def kernel(
    x_ref,
    top_ref,
    ids_ref,
    gain_ref,
    router_ref,
    wg_ref,
    wu_ref,
    wd_ref,
    out_ref,
    wcat,
    wdown,
    swap,
    pick,
    code,
    sel,
    selt,
    dy,
    xr,
    dr,
    xs,
    ds,
    flat,
    ap,
    ac,
    hd,
    pm,
    dcat,
    w_sem,
    xn_s,
    xn_r,
    dy_s,
    dy_r,
    d_s,
    d_r,
    c_s,
    c_r,
    tg_s,
):
    inner, width = wd_ref.shape
    section = lax.axis_index("section")
    me = lax.axis_index("expert")
    last = SECTIONS - 1

    def rows(start, size):
        return pl.ds(pl.multiple_of(start, 16), size)

    def one_hot(mask):
        return mask.astype(jnp.float32).astype(jnp.bfloat16)

    def remote(src, dst, ssem, rsem, sec, dev):
        pltpu.make_async_remote_copy(
            src_ref=src,
            dst_ref=dst,
            send_sem=ssem,
            recv_sem=rsem,
            device_id={"section": sec, "expert": dev},
            device_id_type=pl.DeviceIdType.MESH,
        ).start()

    def wait_bytes(ref, sem):
        pltpu.make_async_copy(ref, ref, sem).wait()

    def exchange(src, dst, ssem, rsem):
        to = dst.at[rows(me * PART, PART)]

        @pl.loop(1, EXPERTS)
        def _(j):
            e = (me + j) % EXPERTS
            remote(src.at[rows(e * PART, PART)], to, ssem, rsem, section, e)

        pltpu.make_async_copy(src.at[rows(me * PART, PART)], to, rsem).start()

    sent = pl.ds(0, ROWS - PART)

    def by_token(values):
        return values.astype(jnp.float32).reshape(TOK, TILE, LANES)

    def mean_of(values):
        return jnp.sum(values, axis=(1, 2), keepdims=True) * (1.0 / width)

    def inverse_of(xf):
        return lax.rsqrt(mean_of(xf * xf) + 1e-05)

    def pack(k, block, stage):
        @pl.loop(0, ROWS // 512)
        def _(n):
            part = rows(n * 512, 512)
            stage[k % 2, part, :] = jnp.dot(
                sel[k, part, :], block, preferred_element_type=jnp.float32
            ).astype(jnp.bfloat16)

    def select(k):
        ids = ids_ref[k]
        lane = lax.broadcasted_iota(jnp.int32, (TOK, LANES), 1)
        named = jnp.zeros((TOK, LANES), jnp.float32)
        for choice in range(ids.shape[1]):
            named = jnp.where(ids[:, choice : choice + 1] == lane, 1.0, named)
        here = lax.broadcasted_iota(jnp.int32, (TOK, TOK), 0)
        other = lax.broadcasted_iota(jnp.int32, (TOK, TOK), 1)
        rank = jnp.dot(
            one_hot(other < here), named.astype(jnp.bfloat16), preferred_element_type=jnp.float32
        )
        first = (named * (TILE * rank + 1.0)).astype(jnp.bfloat16)
        token = lax.broadcasted_iota(jnp.int32, (OWN, TOK), 0) // TILE
        spread = one_hot(token == lax.broadcasted_iota(jnp.int32, (OWN, TOK), 1))
        first = jnp.dot(spread, first, preferred_element_type=jnp.float32)
        offset = lax.broadcasted_iota(jnp.int32, (OWN, LANES), 0) % TILE
        code[k] = jnp.where(first > 0.0, first + offset.astype(jnp.float32), 0.0).astype(
            jnp.bfloat16
        )

        @pl.loop(0, ROWS // 256)
        def _(n):
            part = rows(n * 256, 256)
            held = lax.dot_general(
                pick[part, :], code[k], CONTRACT_LAST, preferred_element_type=jnp.float32
            )
            want = (n * 256 + lax.broadcasted_iota(jnp.int32, (256, OWN), 0)) % PART + 1
            sel[k, part, :] = one_hot(held == want.astype(jnp.float32))

    def select_back(k):
        @pl.loop(0, ROWS // 256)
        def _(n):
            part = pl.ds(pl.multiple_of(n * 256, 256), 256)
            held = lax.dot_general(
                code[k], pick[part, :], CONTRACT_LAST, preferred_element_type=jnp.float32
            )
            want = (n * 256 + lax.broadcasted_iota(jnp.int32, (OWN, 256), 1)) % PART + 1
            selt[k % 2, :, part] = one_hot(held == want.astype(jnp.float32))

    def flatten(tiles, k):
        @pl.loop(0, SLOTS // 16)
        def _(n):
            turned = jnp.dot(
                swap[...], tiles[k, rows(n * 256, 256), :], preferred_element_type=jnp.float32
            ).astype(jnp.bfloat16)
            for j in range(TILE):
                flat[rows(n * 16, 16), pl.ds(j * LANES, LANES)] = turned[j * 16 : (j + 1) * 16]

    def unflatten(tiles, k):
        @pl.loop(0, SLOTS // 16)
        def _(n):
            stacked = jnp.concatenate(
                [flat[rows(n * 16, 16), pl.ds(j * LANES, LANES)] for j in range(TILE)], axis=0
            )
            tiles[k, rows(n * 256, 256), :] = jnp.dot(
                swap[...], stacked, preferred_element_type=jnp.float32
            ).astype(jnp.bfloat16)

    def send_normed(k):
        select(k)

        @pl.when(k >= 2)
        def _():
            wait_bytes(xs.at[0, sent], xn_s.at[k - 2])

        xf = by_token(x_ref[k])
        normed = (xf * inverse_of(xf) * gain_ref[...]).reshape(OWN, LANES).astype(jnp.bfloat16)
        pack(k, normed, xs)
        exchange(xs.at[k % 2], xr.at[k], xn_s.at[k], xn_r.at[k])

    def forward(k):
        wait_bytes(xr.at[k], xn_r.at[k])
        flatten(xr, k)
        logits = jnp.dot(
            flat[...], wcat[:, pl.ds(2 * inner, LANES)], preferred_element_type=jnp.float32
        )
        lane = lax.broadcasted_iota(jnp.int32, (SLOTS, LANES), 1)
        raised = jnp.where(lane < EXPERTS, jnp.exp(logits), 0.0)
        probs = raised / jnp.sum(raised, axis=-1, keepdims=True)
        pm[k] = probs
        picked = jnp.sum(jnp.where(lane == me, probs, 0.0), axis=-1, keepdims=True)

        @pl.loop(0, inner // 256)
        def _(n):
            cols = pl.ds(pl.multiple_of(n * 256, 256), 256)
            more = pl.ds(pl.multiple_of(inner + n * 256, 256), 256)
            gate = jnp.dot(flat[...], wcat[:, cols], preferred_element_type=jnp.float32)
            up = jnp.dot(flat[...], wcat[:, more], preferred_element_type=jnp.float32)
            squash = jax.nn.sigmoid(gate)
            active = gate * squash
            hd[k, :, cols] = (active * up).astype(jnp.bfloat16)
            ac[k, :, cols] = (picked * active).astype(jnp.bfloat16)
            ap[k, :, cols] = (picked * up * squash * (1.0 + gate * (1.0 - squash))).astype(
                jnp.bfloat16
            )

    def normed_step(i):
        @pl.when(i < MICRO)
        def _():
            send_normed(i)

        @pl.when(jnp.logical_and(i >= 1, i <= MICRO))
        def _():
            forward(i - 1)

    def send_grad(k):
        wait_bytes(dy.at[k], dy_r.at[k])

        @pl.when(k >= 2)
        def _():
            wait_bytes(ds.at[0, sent], d_s.at[k - 2])

        pack(k, dy[k], ds)
        exchange(ds.at[k % 2], dr.at[k], d_s.at[k], d_r.at[k])
        select_back(k)

    def backward(k):
        wait_bytes(dr.at[k], d_r.at[k])
        flatten(dr, k)

        def part(n, dprob):
            cols = pl.ds(pl.multiple_of(n * 256, 256), 256)
            more = pl.ds(pl.multiple_of(inner + n * 256, 256), 256)
            dh = lax.dot_general(
                flat[...], wdown[cols, :], CONTRACT_LAST, preferred_element_type=jnp.float32
            )
            dcat[:, cols] = (dh * ap[k, :, cols].astype(jnp.float32)).astype(jnp.bfloat16)
            dcat[:, more] = (dh * ac[k, :, cols].astype(jnp.float32)).astype(jnp.bfloat16)
            return dprob + jnp.sum(
                dh * hd[k, :, cols].astype(jnp.float32), axis=-1, keepdims=True
            )

        dprob = lax.fori_loop(0, inner // 256, part, jnp.zeros((SLOTS, 1), jnp.float32))
        lane = lax.broadcasted_iota(jnp.int32, (SLOTS, LANES), 1)
        probs = pm[k]
        own = jnp.where(lane == me, 1.0, 0.0)
        picked = jnp.sum(probs * own, axis=-1, keepdims=True)
        dcat[:, pl.ds(2 * inner, LANES)] = (picked * dprob * (own - probs)).astype(jnp.bfloat16)

        @pl.loop(0, width // 256)
        def _(n):
            cols = pl.ds(pl.multiple_of(n * 256, 256), 256)
            flat[:, cols] = lax.dot_general(
                dcat[...], wcat[cols, :], CONTRACT_LAST, preferred_element_type=jnp.float32
            ).astype(jnp.bfloat16)

        unflatten(dr, k)
        exchange(dr.at[k], xr.at[k], c_s.at[k], c_r.at[k])

    def finish(k):
        wait_bytes(xr.at[k], c_r.at[k])
        dxn = by_token(jnp.dot(selt[k % 2], xr[k], preferred_element_type=jnp.float32))
        xf = by_token(x_ref[k])
        inv = inverse_of(xf)
        scaled = gain_ref[...] * dxn
        mean = mean_of(xf * scaled)
        grad = by_token(dy[k]) + inv * scaled - xf * (inv * inv * inv * mean)
        out_ref[k] = grad.reshape(OWN, LANES).astype(jnp.bfloat16)

        @pl.when(section > 0)
        def _():
            remote(out_ref.at[k], dy.at[k], dy_s.at[k], dy_r.at[k], section - 1, me)

    for half in range(2):
        at = section * 2 + half

        @pl.when(section == last)
        def _():
            pltpu.make_async_copy(top_ref.at[half], dy.at[at], dy_r.at[at]).start()

        @pl.when(section < last)
        def _():
            remote(top_ref.at[half], dy.at[at], tg_s.at[half], dy_r.at[at], last, me)

    weights = [
        pltpu.make_async_copy(wg_ref, wcat.at[:, pl.ds(0, inner)], w_sem.at[0]),
        pltpu.make_async_copy(wu_ref, wcat.at[:, pl.ds(inner, inner)], w_sem.at[1]),
        pltpu.make_async_copy(router_ref, wcat.at[:, pl.ds(2 * inner, LANES)], w_sem.at[2]),
        pltpu.make_async_copy(wd_ref, wdown, w_sem.at[3]),
    ]
    for copy in weights:
        copy.start()

    here = lax.broadcasted_iota(jnp.int32, (256, 256), 0)
    other = lax.broadcasted_iota(jnp.int32, (256, 256), 1)
    swap[...] = one_hot(
        jnp.logical_and(here % TILE == other // TILE, here // TILE == other % TILE)
    )
    expert = lax.broadcasted_iota(jnp.int32, (ROWS, LANES), 0) // PART
    pick[...] = one_hot(expert == lax.broadcasted_iota(jnp.int32, (ROWS, LANES), 1))
    normed_step(0)
    for copy in weights:
        copy.wait()

    ahead = jnp.where(section == last, AHEAD_LAST, MICRO)

    @pl.loop(1, ahead + 1)
    def _(i):
        normed_step(i)

    @pl.loop(0, MICRO + 1)
    def _(k):
        @pl.when(k < MICRO)
        def _():
            send_grad(k)

        normed_step(k + ahead + 1)

        @pl.when(k >= 1)
        def _():
            finish(k - 1)

        @pl.when(k < MICRO)
        def _():
            backward(k)

    @pl.loop(MICRO - 2, MICRO)
    def _(k):
        wait_bytes(xs.at[0, sent], xn_s.at[k])
        wait_bytes(ds.at[0, sent], d_s.at[k])

    @pl.loop(0, MICRO)
    def _(k):
        wait_bytes(xs.at[0, sent], c_s.at[k])

        @pl.when(section > 0)
        def _():
            wait_bytes(dy.at[0], dy_s.at[k])

    for half in range(2):

        @pl.when(section < last)
        def _():
            wait_bytes(dy.at[0], tg_s.at[half])


def shards(layer_inputs, top_grad, expert_ids, router, norm_gain, w_gate, w_up, w_down):
    width = layer_inputs.shape[3]
    inner = w_down.shape[2]
    padded = jnp.pad(router[0], ((0, 0), (0, LANES - EXPERTS)))
    vmem = pl.BlockSpec(memory_space=pltpu.VMEM)
    hbm = pl.BlockSpec(memory_space=pl.ANY)
    half = jnp.bfloat16
    tiles = (MICRO, ROWS, LANES)
    factor = (MICRO, SLOTS, inner)
    dma = pltpu.SemaphoreType.DMA
    out = pl.pallas_call(
        kernel,
        out_shape=jax.ShapeDtypeStruct((MICRO, OWN, LANES), half),
        in_specs=[vmem] * 4 + [hbm] * 4,
        out_specs=vmem,
        scratch_shapes=[
            pltpu.VMEM((width, 2 * inner + LANES), half),
            pltpu.VMEM((inner, width), half),
            pltpu.VMEM((256, 256), half),
            pltpu.VMEM((ROWS, LANES), half),
            pltpu.VMEM((MICRO, OWN, LANES), half),
            pltpu.VMEM((MICRO, ROWS, OWN), half),
            pltpu.VMEM((2, OWN, ROWS), half),
            pltpu.VMEM((MICRO, OWN, LANES), half),
            pltpu.VMEM(tiles, half),
            pltpu.VMEM(tiles, half),
            pltpu.VMEM((2, ROWS, LANES), half),
            pltpu.VMEM((2, ROWS, LANES), half),
            pltpu.VMEM((SLOTS, width), half),
            pltpu.VMEM(factor, half),
            pltpu.VMEM(factor, half),
            pltpu.VMEM(factor, half),
            pltpu.VMEM((MICRO, SLOTS, LANES), jnp.float32),
            pltpu.VMEM((SLOTS, 2 * inner + LANES), half),
            dma((4,)),
        ]
        + [dma((MICRO,)) for _ in range(8)]
        + [dma((2,))],
        compiler_params=pltpu.CompilerParams(
            has_side_effects=True, vmem_limit_bytes=60 * 1024 * 1024
        ),
    )(
        layer_inputs[0].reshape(MICRO, OWN, LANES),
        top_grad.reshape(2, OWN, LANES),
        expert_ids[0],
        norm_gain.astype(jnp.float32).reshape(1, TILE, LANES),
        padded,
        w_gate[0, 0],
        w_up[0, 0],
        w_down[0, 0],
    )
    return out.reshape(1, MICRO, TOK, width)


def solution(mesh):
    placed = (
        P("section", None, "expert", None),
        P("section", "expert", None),
        P("section", None, "expert", None),
        P("section", None, None),
        P("section", None),
        P("section", "expert", None, None),
        P("section", "expert", None, None),
        P("section", "expert", None, None),
    )
    return jax.shard_map(
        shards,
        mesh=mesh,
        in_specs=placed,
        out_specs=P("section", None, "expert", None),
        check_vma=False,
    )
```

time: 414 us -> 357 us (0.86)
  Pallas kernels: 407 us -> 346 us
    pallas_call x1, Pallas kernels: 407 us -> 346 us  [shards(): pl.pallas_call(kernel, out_shape=jax.ShapeDtypeStruct((MICRO, OWN, LANES)...]
where the time goes in v3:
time: 357 us
  Pallas kernels  346 us (97%)
  local copies, waits for them, and re-layouts  9.28 us (3%)
    pallas_call x1, Pallas kernels, shards(): pl.pallas_call(kernel, out_shape=jax.ShapeDtypeStruct((MICRO, OWN, LANES)...  346 us

profile of v3, /device:TPU:0, one launch (start us, length us, event | category | flops | bytes accessed | tf_op | source)
XLA Modules:
  0.0 356.9 jit_solution(18375499342526239716)
XLA Ops:
  0.0 1.3 reshape.15
  1.3 1.5 copy.9
  2.8 1.6 reshape.11.top_ref
  4.4 2.1 reshape_squeeze.3.x_ref
  6.4 1.2 copy.10
  7.6 0.9 pad.4.router_ref
  8.5 346.3 %shard_map.82 = bf16[8,256,128]{2,1,0:T(8,128)(2,1)} custom-call(bf16[8,256,128]{2,1,0:T(8,128)(2,1)} %reshape_squeeze.3.x_ref, bf16[2,256,128]{2,1,0:T(8,128)(2,1)} %reshape.11.top_ref, s32[8,16,8]{2,1,0:T(8,128)} %bitcast.12, f32[1,16,128]{2,1,0:T(8,128)} %bitcast.13, bf16[2048,128]{1,0:T(8,128)(2,1)} %pad.4.router_ref, bf16[2048,1024]{1,0:T(8,128)(2,1)} %bitcast.8, ...), custom_call_target="tpu_custom_call" | custom-call | tf_op jit(solution)/shard_map/pallas_call | solution.py:361
  354.9 2.1 reshape.14

commit v4 on v3

--- a/solution.py
+++ b/solution.py
@@ -16,7 +16,6 @@
 PART = MOST * TILE
 ROWS = SLOTS * TILE
 OWN = TOK * TILE
-AHEAD_LAST = 2
 CONTRACT_LAST = (((1,), (1,)), ((), ()))
 
 
@@ -31,8 +30,13 @@
     wd_ref,
     out_ref,
     wcat,
+    wback,
     wdown,
     swap,
+    same,
+    xt,
+    tt,
+    gt,
     pick,
     code,
     sel,
@@ -95,6 +99,11 @@
 
     sent = pl.ds(0, ROWS - PART)
 
+    def tiles_of(pieces):
+        return jnp.dot(
+            swap[...], jnp.concatenate(pieces, axis=0), preferred_element_type=jnp.float32
+        ).astype(jnp.bfloat16)
+
     def by_token(values):
         return values.astype(jnp.float32).reshape(TOK, TILE, LANES)
 
@@ -105,7 +114,7 @@
         return lax.rsqrt(mean_of(xf * xf) + 1e-05)
 
     def pack(k, block, stage):
-        @pl.loop(0, ROWS // 512)
+        @pl.loop(0, ROWS // 512, unroll=True)
         def _(n):
             part = rows(n * 512, 512)
             stage[k % 2, part, :] = jnp.dot(
@@ -114,12 +123,18 @@
 
     def select(k):
         ids = ids_ref[k]
-        lane = lax.broadcasted_iota(jnp.int32, (TOK, LANES), 1)
-        named = jnp.zeros((TOK, LANES), jnp.float32)
-        for choice in range(ids.shape[1]):
-            named = jnp.where(ids[:, choice : choice + 1] == lane, 1.0, named)
+        number = lax.broadcasted_iota(jnp.int32, (LANES, TOK), 0)
+        turned = jnp.zeros((LANES, TOK), jnp.float32)
+        for choice in range(ids.shape[0]):
+            turned = jnp.where(ids[choice : choice + 1, :] == number, 1.0, turned)
         here = lax.broadcasted_iota(jnp.int32, (TOK, TOK), 0)
         other = lax.broadcasted_iota(jnp.int32, (TOK, TOK), 1)
+        named = lax.dot_general(
+            one_hot(other == here),
+            turned.astype(jnp.bfloat16),
+            CONTRACT_LAST,
+            preferred_element_type=jnp.float32,
+        )
         rank = jnp.dot(
             one_hot(other < here), named.astype(jnp.bfloat16), preferred_element_type=jnp.float32
         )
@@ -128,31 +143,29 @@
         spread = one_hot(token == lax.broadcasted_iota(jnp.int32, (OWN, TOK), 1))
         first = jnp.dot(spread, first, preferred_element_type=jnp.float32)
         offset = lax.broadcasted_iota(jnp.int32, (OWN, LANES), 0) % TILE
-        code[k] = jnp.where(first > 0.0, first + offset.astype(jnp.float32), 0.0).astype(
-            jnp.bfloat16
-        )
-
-        @pl.loop(0, ROWS // 256)
+        found = jnp.where(first > 0.0, first + offset.astype(jnp.float32), 0.0)
+        lane = lax.broadcasted_iota(jnp.int32, (OWN, LANES), 1)
+        code[k] = jnp.where(lane == EXPERTS, 1.0, found).astype(jnp.bfloat16)
+
+        @pl.loop(0, ROWS // 256, unroll=5)
         def _(n):
             part = rows(n * 256, 256)
             held = lax.dot_general(
                 pick[part, :], code[k], CONTRACT_LAST, preferred_element_type=jnp.float32
             )
-            want = (n * 256 + lax.broadcasted_iota(jnp.int32, (256, OWN), 0)) % PART + 1
-            sel[k, part, :] = one_hot(held == want.astype(jnp.float32))
+            sel[k, part, :] = one_hot(held == 0.0)
 
     def select_back(k):
-        @pl.loop(0, ROWS // 256)
+        @pl.loop(0, ROWS // 256, unroll=5)
         def _(n):
             part = pl.ds(pl.multiple_of(n * 256, 256), 256)
             held = lax.dot_general(
                 code[k], pick[part, :], CONTRACT_LAST, preferred_element_type=jnp.float32
             )
-            want = (n * 256 + lax.broadcasted_iota(jnp.int32, (OWN, 256), 1)) % PART + 1
-            selt[k % 2, :, part] = one_hot(held == want.astype(jnp.float32))
+            selt[k % 2, :, part] = one_hot(held == 0.0)
 
     def flatten(tiles, k):
-        @pl.loop(0, SLOTS // 16)
+        @pl.loop(0, SLOTS // 16, unroll=5)
         def _(n):
             turned = jnp.dot(
                 swap[...], tiles[k, rows(n * 256, 256), :], preferred_element_type=jnp.float32
@@ -161,14 +174,11 @@
                 flat[rows(n * 16, 16), pl.ds(j * LANES, LANES)] = turned[j * 16 : (j + 1) * 16]
 
     def unflatten(tiles, k):
-        @pl.loop(0, SLOTS // 16)
-        def _(n):
-            stacked = jnp.concatenate(
-                [flat[rows(n * 16, 16), pl.ds(j * LANES, LANES)] for j in range(TILE)], axis=0
+        @pl.loop(0, SLOTS // 16, unroll=5)
+        def _(n):
+            tiles[k, rows(n * 256, 256), :] = tiles_of(
+                [flat[rows(n * 16, 16), pl.ds(j * LANES, LANES)] for j in range(TILE)]
             )
-            tiles[k, rows(n * 256, 256), :] = jnp.dot(
-                swap[...], stacked, preferred_element_type=jnp.float32
-            ).astype(jnp.bfloat16)
 
     def send_normed(k):
         select(k)
@@ -177,16 +187,20 @@
         def _():
             wait_bytes(xs.at[0, sent], xn_s.at[k - 2])
 
-        xf = by_token(x_ref[k])
-        normed = (xf * inverse_of(xf) * gain_ref[...]).reshape(OWN, LANES).astype(jnp.bfloat16)
+        xt[k] = tiles_of([x_ref[k, :, pl.ds(j * LANES, LANES)] for j in range(TILE)])
+        xf = by_token(xt[k])
+        normed = (xf * inverse_of(xf) * gt[...][None]).reshape(OWN, LANES).astype(jnp.bfloat16)
         pack(k, normed, xs)
         exchange(xs.at[k % 2], xr.at[k], xn_s.at[k], xn_r.at[k])
 
     def forward(k):
         wait_bytes(xr.at[k], xn_r.at[k])
         flatten(xr, k)
-        logits = jnp.dot(
-            flat[...], wcat[:, pl.ds(2 * inner, LANES)], preferred_element_type=jnp.float32
+        logits = lax.dot_general(
+            flat[...],
+            wback[pl.ds(2 * inner, LANES), :],
+            CONTRACT_LAST,
+            preferred_element_type=jnp.float32,
         )
         lane = lax.broadcasted_iota(jnp.int32, (SLOTS, LANES), 1)
         raised = jnp.where(lane < EXPERTS, jnp.exp(logits), 0.0)
@@ -235,9 +249,7 @@
         def part(n, dprob):
             cols = pl.ds(pl.multiple_of(n * 256, 256), 256)
             more = pl.ds(pl.multiple_of(inner + n * 256, 256), 256)
-            dh = lax.dot_general(
-                flat[...], wdown[cols, :], CONTRACT_LAST, preferred_element_type=jnp.float32
-            )
+            dh = jnp.dot(flat[...], wdown[:, cols], preferred_element_type=jnp.float32)
             dcat[:, cols] = (dh * ap[k, :, cols].astype(jnp.float32)).astype(jnp.bfloat16)
             dcat[:, more] = (dh * ac[k, :, cols].astype(jnp.float32)).astype(jnp.bfloat16)
             return dprob + jnp.sum(
@@ -254,8 +266,8 @@
         @pl.loop(0, width // 256)
         def _(n):
             cols = pl.ds(pl.multiple_of(n * 256, 256), 256)
-            flat[:, cols] = lax.dot_general(
-                dcat[...], wcat[cols, :], CONTRACT_LAST, preferred_element_type=jnp.float32
+            flat[:, cols] = jnp.dot(
+                dcat[...], wback[:, cols], preferred_element_type=jnp.float32
             ).astype(jnp.bfloat16)
 
         unflatten(dr, k)
@@ -264,9 +276,9 @@
     def finish(k):
         wait_bytes(xr.at[k], c_r.at[k])
         dxn = by_token(jnp.dot(selt[k % 2], xr[k], preferred_element_type=jnp.float32))
-        xf = by_token(x_ref[k])
+        xf = by_token(xt[k])
         inv = inverse_of(xf)
-        scaled = gain_ref[...] * dxn
+        scaled = gt[...][None] * dxn
         mean = mean_of(xf * scaled)
         grad = by_token(dy[k]) + inv * scaled - xf * (inv * inv * inv * mean)
         out_ref[k] = grad.reshape(OWN, LANES).astype(jnp.bfloat16)
@@ -275,22 +287,29 @@
         def _():
             remote(out_ref.at[k], dy.at[k], dy_s.at[k], dy_r.at[k], section - 1, me)
 
-    for half in range(2):
-        at = section * 2 + half
-
-        @pl.when(section == last)
-        def _():
-            pltpu.make_async_copy(top_ref.at[half], dy.at[at], dy_r.at[at]).start()
-
-        @pl.when(section < last)
-        def _():
-            remote(top_ref.at[half], dy.at[at], tg_s.at[half], dy_r.at[at], last, me)
+    def turn_weights():
+        @pl.loop(0, inner // 256)
+        def _(n):
+            part = pl.ds(pl.multiple_of(n * 256, 256), 256)
+            for m in range(width // 256):
+                other = pl.ds(m * 256, 256)
+                wdown[other, part] = lax.dot_general(
+                    same[...], wback[part, other], CONTRACT_LAST, preferred_element_type=jnp.float32
+                ).astype(jnp.bfloat16)
+
+        @pl.loop(0, 2 * inner // 256)
+        def _(n):
+            part = pl.ds(pl.multiple_of(n * 256, 256), 256)
+            for m in range(width // 256):
+                other = pl.ds(m * 256, 256)
+                wback[part, other] = lax.dot_general(
+                    same[...], wcat[other, part], CONTRACT_LAST, preferred_element_type=jnp.float32
+                ).astype(jnp.bfloat16)
 
     weights = [
         pltpu.make_async_copy(wg_ref, wcat.at[:, pl.ds(0, inner)], w_sem.at[0]),
         pltpu.make_async_copy(wu_ref, wcat.at[:, pl.ds(inner, inner)], w_sem.at[1]),
-        pltpu.make_async_copy(router_ref, wcat.at[:, pl.ds(2 * inner, LANES)], w_sem.at[2]),
-        pltpu.make_async_copy(wd_ref, wdown, w_sem.at[3]),
+        pltpu.make_async_copy(wd_ref, wback.at[pl.ds(0, inner), :], w_sem.at[2]),
     ]
     for copy in weights:
         copy.start()
@@ -300,17 +319,42 @@
     swap[...] = one_hot(
         jnp.logical_and(here % TILE == other // TILE, here // TILE == other % TILE)
     )
-    expert = lax.broadcasted_iota(jnp.int32, (ROWS, LANES), 0) // PART
-    pick[...] = one_hot(expert == lax.broadcasted_iota(jnp.int32, (ROWS, LANES), 1))
-    normed_step(0)
-    for copy in weights:
-        copy.wait()
-
-    ahead = jnp.where(section == last, AHEAD_LAST, MICRO)
-
-    @pl.loop(1, ahead + 1)
+    same[...] = one_hot(here == other)
+    for half in range(2):
+        at = section * 2 + half
+        tt[half] = tiles_of([top_ref[half, :, pl.ds(j * LANES, LANES)] for j in range(TILE)])
+
+        @pl.when(section == last)
+        def _():
+            pltpu.make_async_copy(tt.at[half], dy.at[at], dy_r.at[at]).start()
+
+        @pl.when(section < last)
+        def _():
+            remote(tt.at[half], dy.at[at], tg_s.at[half], dy_r.at[at], last, me)
+
+    wback[pl.ds(2 * inner, EXPERTS), :] = router_ref[...]
+    wback[pl.ds(2 * inner + EXPERTS, LANES - EXPERTS), :] = jnp.zeros(
+        (LANES - EXPERTS, width), jnp.bfloat16
+    )
+    for j in range(TILE):
+        gt[pl.ds(j, 1), :] = gain_ref[:, pl.ds(j * LANES, LANES)].astype(jnp.float32)
+    for e in range(EXPERTS):
+        lane = lax.broadcasted_iota(jnp.int32, (PART, LANES), 1)
+        place = lax.broadcasted_iota(jnp.int32, (PART, LANES), 0).astype(jnp.float32)
+        pick[pl.ds(e * PART, PART), :] = jnp.where(
+            lane == EXPERTS, -1.0 - place, jnp.where(lane == e, 1.0, 0.0)
+        ).astype(jnp.bfloat16)
+    ahead = jnp.where(section == last, 1, jnp.where(section == last - 1, 3, MICRO))
+
+    @pl.loop(0, ahead + 1)
     def _(i):
         normed_step(i)
+
+        @pl.when(i == 0)
+        def _():
+            for copy in weights:
+                copy.wait()
+            turn_weights()
 
     @pl.loop(0, MICRO + 1)
     def _(k):
@@ -318,11 +362,11 @@
         def _():
             send_grad(k)
 
+        @pl.when(k >= 1)
+        def _():
+            finish(k - 1)
+
         normed_step(k + ahead + 1)
-
-        @pl.when(k >= 1)
-        def _():
-            finish(k - 1)
 
         @pl.when(k < MICRO)
         def _():
@@ -351,7 +395,6 @@
 def shards(layer_inputs, top_grad, expert_ids, router, norm_gain, w_gate, w_up, w_down):
     width = layer_inputs.shape[3]
     inner = w_down.shape[2]
-    padded = jnp.pad(router[0], ((0, 0), (0, LANES - EXPERTS)))
     vmem = pl.BlockSpec(memory_space=pltpu.VMEM)
     hbm = pl.BlockSpec(memory_space=pl.ANY)
     half = jnp.bfloat16
@@ -361,12 +404,17 @@
     out = pl.pallas_call(
         kernel,
         out_shape=jax.ShapeDtypeStruct((MICRO, OWN, LANES), half),
-        in_specs=[vmem] * 4 + [hbm] * 4,
+        in_specs=[vmem] * 5 + [hbm] * 3,
         out_specs=vmem,
         scratch_shapes=[
-            pltpu.VMEM((width, 2 * inner + LANES), half),
-            pltpu.VMEM((inner, width), half),
+            pltpu.VMEM((width, 2 * inner), half),
+            pltpu.VMEM((2 * inner + LANES, width), half),
+            pltpu.VMEM((width, inner), half),
             pltpu.VMEM((256, 256), half),
+            pltpu.VMEM((256, 256), half),
+            pltpu.VMEM((MICRO, OWN, LANES), half),
+            pltpu.VMEM((2, OWN, LANES), half),
+            pltpu.VMEM((TILE, LANES), jnp.float32),
             pltpu.VMEM((ROWS, LANES), half),
             pltpu.VMEM((MICRO, OWN, LANES), half),
             pltpu.VMEM((MICRO, ROWS, OWN), half),
@@ -382,7 +430,7 @@
             pltpu.VMEM(factor, half),
             pltpu.VMEM((MICRO, SLOTS, LANES), jnp.float32),
             pltpu.VMEM((SLOTS, 2 * inner + LANES), half),
-            dma((4,)),
+            dma((3,)),
         ]
         + [dma((MICRO,)) for _ in range(8)]
         + [dma((2,))],
@@ -390,11 +438,11 @@
             has_side_effects=True, vmem_limit_bytes=60 * 1024 * 1024
         ),
     )(
-        layer_inputs[0].reshape(MICRO, OWN, LANES),
-        top_grad.reshape(2, OWN, LANES),
-        expert_ids[0],
-        norm_gain.astype(jnp.float32).reshape(1, TILE, LANES),
-        padded,
+        layer_inputs[0],
+        top_grad,
+        jnp.transpose(expert_ids[0], (0, 2, 1)),
+        norm_gain,
+        jnp.transpose(router[0]),
         w_gate[0, 0],
         w_up[0, 0],
         w_down[0, 0],

time: 357 us -> 310 us (0.87)
  Pallas kernels: 346 us -> 308 us
  local copies, waits for them, and re-layouts: 9.28 us -> 2.06 us
    pallas_call x1, Pallas kernels: 346 us -> 308 us  [shards(): pl.pallas_call(kernel, out_shape=jax.ShapeDtypeStruct((MICRO, OWN, LANES)...]
where the time goes in v4:
time: 310 us
  Pallas kernels  308 us (99%)
    pallas_call x1, Pallas kernels, shards(): pl.pallas_call(kernel, out_shape=jax.ShapeDtypeStruct((MICRO, OWN, LANES)...  308 us

profile of v4, /device:TPU:0, one launch (start us, length us, event | category | flops | bytes accessed | tf_op | source)
XLA Modules:
  0.0 309.9 jit_solution(17372850326066099120)
XLA Ops:
  0.0 307.9 %shard_map.82 = bf16[8,256,128]{2,1,0:T(8,128)(2,1)} custom-call(bf16[8,16,2048]{2,1,0:T(8,128)(2,1)} %bitcast.13, bf16[2,16,2048]{2,1,0:T(8,128)(2,1)} %top_ref.1, s32[8,8,16]{2,1,0:T(8,128)} %bitcast.15, bf16[1,2048]{1,0:T(2,128)(2,1)} %gain_ref.1, bf16[32,2048]{1,0:T(8,128)(2,1)} %bitcast.14, bf16[2048,1024]{1,0:T(8,128)(2,1)} %bitcast.10, ...), custom_call_target="tpu_custom_call" | custom-call | tf_op jit(solution)/shard_map/pallas_call | solution.py:404
  307.9 2.1 reshape.3

commit v5 on v4

--- a/solution.py
+++ b/solution.py
@@ -362,11 +362,11 @@
         def _():
             send_grad(k)
 
+        normed_step(k + ahead + 1)
+
         @pl.when(k >= 1)
         def _():
             finish(k - 1)
-
-        normed_step(k + ahead + 1)
 
         @pl.when(k < MICRO)
         def _():

time: 310 us -> 295 us (0.952)
  Pallas kernels: 308 us -> 292 us
    pallas_call x1, Pallas kernels: 308 us -> 292 us  [shards(): pl.pallas_call(kernel, out_shape=jax.ShapeDtypeStruct((MICRO, OWN, LANES)...]
where the time goes in v5:
time: 295 us; the launch traced here: 294 us
  Pallas kernels  292 us (99%)
    pallas_call x1, Pallas kernels, shards(): pl.pallas_call(kernel, out_shape=jax.ShapeDtypeStruct((MICRO, OWN, LANES)...  292 us

profile of v5, /device:TPU:0, one launch (start us, length us, event | category | flops | bytes accessed | tf_op | source)
XLA Modules:
  0.0 294.3 jit_solution(14684072968606567056)
XLA Ops:
  0.0 292.3 %shard_map.82 = bf16[8,256,128]{2,1,0:T(8,128)(2,1)} custom-call(bf16[8,16,2048]{2,1,0:T(8,128)(2,1)} %bitcast.13, bf16[2,16,2048]{2,1,0:T(8,128)(2,1)} %top_ref.1, s32[8,8,16]{2,1,0:T(8,128)} %bitcast.15, bf16[1,2048]{1,0:T(2,128)(2,1)} %gain_ref.1, bf16[32,2048]{1,0:T(8,128)(2,1)} %bitcast.14, bf16[2048,1024]{1,0:T(8,128)(2,1)} %bitcast.10, ...), custom_call_target="tpu_custom_call" | custom-call | tf_op jit(solution)/shard_map/pallas_call | solution.py:404
  292.3 2.1 reshape.3
